TPU v7x, 256 devices: a whole 4x4x8 slice. The times are simulated.
256 devices in a mesh: heads: 8 (over y, core), seq: 32 (over x, z).
Axes of the slice: x: 4, y: 4, z: 8, core: 2. Of those that a mesh axis runs over, the one named last changes fastest.
Arguments:
- queries: bfloat16 [8192, 1024], P(('seq', 'heads')), may hold values from -0.75 to 0.75
- keys: bfloat16 [8192, 1024], P(('seq', 'heads')), may hold values from -0.75 to 0.75
- values: bfloat16 [8192, 1024], P(('seq', 'heads')), may hold values from -6 to 6
- out_grad: bfloat16 [8192, 1024], P(('seq', 'heads')), may hold values from -0.0625 to 0.0625
- prefix_state: bfloat16 [32, 2080, 1024], P('seq', None, 'heads'), may hold values from -48 to 48
- variant_queries: bfloat16 [256, 1024], P('seq', 'heads'), may hold values from -0.75 to 0.75
- variant_grads: bfloat16 [256, 1024], P('seq', 'heads'), may hold values from -0.25 to 0.25
- variant_owner: int32 [256], replicated, may hold values from 0 to 31
- variant_position: int32 [256], replicated, may hold values from 0 to 255
- doc_start: int32 [32], P('seq'), may hold values from 1 to 256, as said below
Outputs:
- query_grad: float32 [8192, 1024], P(('seq', 'heads'))
- key_grad: float32 [8192, 1024], P(('seq', 'heads'))
- value_grad: float32 [8192, 1024], P(('seq', 'heads'))
Inputs may be any that keep to these rules, and one draw needn't show every extreme that they name: `doc_start`: a document starts at this local position of the shard; 256 means that none starts inside it. `variant_position`: the local position in that shard at which the variant row stands.
All inputs are finite; a program needn't handle non-finite values.
Results may differ from a plain program's by a relative error of at most 0.004.
Values may be sent and summed in bfloat16 or wider, within the bound.
No kernel may reach another device: no remote copies, remote signals or barrier semaphores. Data moves between devices by JAX's collectives and lax.ppermute only.
A program may use at most 128 MiB of HBM per device.

v0:
```python
import functools
import math

import jax
import jax.numpy as jnp
from jax import lax
from jax.experimental import pallas as pl
from jax.experimental.pallas import tpu as pltpu
from jax.sharding import PartitionSpec as P

HEAD = 64
PAIR = 128
TOK = 256
FEAT = 2080
SHARDS = 32
ROW = 8
COLS = SHARDS // ROW
REACH = 10
F32 = jnp.float32
BF16 = jnp.bfloat16
I32 = jnp.int32

VMEM = pl.BlockSpec(memory_space=pltpu.VMEM)
SMEM = pl.BlockSpec(memory_space=pltpu.SMEM)


def call(body, out_shape, in_specs, out_specs, flops, scratch=(), aliases=None, name=None,
         vmem=24):
    return pl.pallas_call(
        body,
        out_shape=out_shape,
        in_specs=in_specs,
        out_specs=out_specs,
        scratch_shapes=list(scratch),
        input_output_aliases=aliases or {},
        compiler_params=pltpu.CompilerParams(vmem_limit_bytes=vmem * 1024 * 1024),
        cost_estimate=pl.CostEstimate(flops=flops, bytes_accessed=1 << 20, transcendentals=0),
        name=name,
    )


def dot_nt(a, b):
    return lax.dot_general(a, b, (((1,), (1,)), ((), ())), preferred_element_type=F32)


def dot_tn(a, b):
    return lax.dot_general(a, b, (((0,), (0,)), ((), ())), preferred_element_type=F32)


def dot_nn(a, b):
    return lax.dot_general(a, b, (((1,), (0,)), ((), ())), preferred_element_type=F32)


def by_head(x):
    low = lax.broadcasted_iota(I32, x.shape, 1) < HEAD
    zero = jnp.zeros_like(x)
    return jnp.where(low, x, zero), jnp.where(low, zero, x)


def attend(q, g, keys, values, lo, hi):
    place = lax.broadcasted_iota(I32, (TOK, q.shape[0]), 0)
    seen = (place >= lo) & (place <= hi)
    slopes, squares = [], []
    for k, v in zip(by_head(keys), by_head(values)):
        score = jnp.where(seen, dot_nt(k, q), 0.0)
        inner = dot_nt(v, g)
        slopes.append((2.0 * score * inner).astype(BF16))
        squares.append((score * score).astype(BF16))
    slope = jnp.concatenate(slopes, 1)
    square = jnp.concatenate(squares, 1)
    k_part = dot_nn(slope, jnp.concatenate(by_head(q), 0))
    v_part = dot_nn(square, jnp.concatenate(by_head(g), 0))
    return slopes, k_part, v_part


def pack_body(start, q, g, k, v, vq, vg, out, msg, buf, sems):
    copies = [
        pltpu.make_async_copy(ref, buf.at[n], sems.at[n]) for n, ref in enumerate((q, g, k, v))
    ]
    for copy in copies:
        copy.start()
    top = jnp.concatenate([vq[...], vg[...]], 1).astype(F32)
    low = jnp.full((8, 2 * PAIR), start[0].astype(F32))
    msg[...] = jnp.concatenate([top, low], 0).astype(BF16)
    for n, copy in enumerate(copies):
        copy.wait()
        for h in range(out.shape[0]):
            out[h, :, n * PAIR : (n + 1) * PAIR] = buf[n, :, h * PAIR : (h + 1) * PAIR]


def unpack_body(x, qo, ko, vo):
    for h in range(x.shape[0]):
        for n, ref in enumerate((qo, ko, vo)):
            ref[:, h * PAIR : (h + 1) * PAIR] = x[h, :, n * PAIR : (n + 1) * PAIR].astype(F32)


def assemble_body(t, *rest):
    msgs, (block, rows) = rest[:COLS], rest[COLS:]
    x = lax.div(lax.axis_index("seq"), ROW)
    block[0:TOK, :] = t[:, 0 : 2 * PAIR]
    group = lax.shift_right_logical(lax.broadcasted_iota(I32, (16, 2 * PAIR), 0), 2)
    starts = jnp.zeros((16, 2 * PAIR), F32)
    for dx, msg in enumerate(msgs):
        at = lax.rem(x + dx, COLS)
        piece = msg[...].astype(F32)
        rows[pl.ds(pl.multiple_of(at * 8, 8), 8), :] = piece[0:8, :]
        starts = jnp.where(group == at, piece[8:9, :], starts)
    block[TOK : TOK + 32, :] = rows[...].astype(BF16)
    block[TOK + 32 : TOK + 48, :] = starts.astype(BF16)


def own_body(start_ref, owner, place, t, acc, who):
    who[0:1, :] = owner[...]
    who[1:2, :] = place[...]
    start = start_ref[0]
    spot = lax.broadcasted_iota(I32, (1, TOK), 1)
    lo = jnp.where(spot >= start, start, 0)
    q, g, k, v = (t[:, n * PAIR : (n + 1) * PAIR] for n in range(4))
    slopes, k_part, v_part = attend(q, g, k, v, lo, spot)
    k0, k1 = by_head(k)
    acc[:, 0:PAIR] = dot_tn(slopes[0], k0) + dot_tn(slopes[1], k1)
    acc[:, PAIR : 2 * PAIR] = k_part
    acc[:, 2 * PAIR : 3 * PAIR] = v_part


def state_body(start_ref, m, t, acc_in, acc, pt, qt, rows, res):
    start = start_ref[0]
    chunk = 416
    for h, g in enumerate(by_head(t[:, PAIR : 2 * PAIR])):
        for c in range(0, FEAT, chunk):
            r = dot_nt(m[c : c + chunk, :], g)
            pt[2 * h, c : c + chunk, :] = r[:, 0:PAIR]
            pt[2 * h + 1, c : c + chunk, :] = r[:, PAIR : 2 * PAIR]
    q_t = t[:, 0:PAIR].astype(F32).T
    for h in range(2):
        for half in range(2):
            qt[2 * h + half] = q_t[h * HEAD : (h + 1) * HEAD, half * PAIR : (half + 1) * PAIR]
    sub = lax.broadcasted_iota(I32, (8, PAIR), 0)

    def part(i, carry):
        tiles = HEAD // 8
        sums = [jnp.zeros((8, PAIR), F32) for _ in range(tiles)]
        for a in range(HEAD):
            first = a // 8
            at = a * HEAD - a * (a - 1) // 2 - a % 8
            qa = qt[i, a : a + 1, :]
            row = None
            for b in range(first, tiles):
                tile = pt[i, at + 8 * (b - first) : at + 8 * (b - first) + 8, :]
                if b == first:
                    scale = jnp.where(sub > a % 8, 1.0, jnp.where(sub == a % 8, math.sqrt(0.5), 0.0))
                    tile = tile * scale
                sums[b] = sums[b] + tile * qa
                more = tile * qt[i, 8 * b : 8 * b + 8, :]
                row = more if row is None else row + more
            rows[i, a : a + 1, :] = jnp.sum(row, axis=0, keepdims=True)
        for b in range(tiles):
            res[i, 8 * b : 8 * b + 8, :] = math.sqrt(2.0) * (sums[b] + rows[i, 8 * b : 8 * b + 8, :])
        return carry

    lax.fori_loop(0, 4, part, 0)
    for half in range(2):
        both = jnp.concatenate([res[half], res[2 + half]], 0).T
        spot = half * PAIR + lax.broadcasted_iota(I32, (PAIR, PAIR), 0)
        at = slice(half * PAIR, (half + 1) * PAIR)
        acc[at, 0:PAIR] = acc_in[at, 0:PAIR] + jnp.where(spot < start, both, 0.0)
    acc[:, PAIR : 3 * PAIR] = acc_in[:, PAIR : 3 * PAIR]


def later_part(far, start, t, block):
    x = lax.rem(lax.div(lax.axis_index("seq") + far, ROW), COLS)
    group = lax.shift_right_logical(lax.broadcasted_iota(I32, (16, 2 * PAIR), 0), 2)
    begin = block[TOK + 32 : TOK + 48, :].astype(F32)
    until = jnp.max(jnp.where(group == x, begin, 0.0), axis=0, keepdims=True).astype(I32)
    spot = lax.broadcasted_iota(I32, (1, TOK), 1)
    lo = jnp.where(start == TOK, 0, start)
    hi = jnp.where(spot < until, TOK - 1, -1)
    k, v = t[:, 2 * PAIR : 3 * PAIR], t[:, 3 * PAIR : 4 * PAIR]
    q, g = block[0:TOK, 0:PAIR], block[0:TOK, PAIR : 2 * PAIR]
    _, k_part, v_part = attend(q, g, k, v, lo, hi)
    return k_part, v_part


def later_body(fars, start_ref, t, *rest):
    blocks, out = rest[:-1], rest[-1]
    for n, (far, block) in enumerate(zip(fars, blocks)):
        k_part, v_part = later_part(far, start_ref[0], t, block)
        out[n, :, 0:PAIR] = k_part
        out[n, :, PAIR : 2 * PAIR] = v_part


def add_later(far, count, start, t, block, acc):
    @pl.when(far <= count)
    def _():
        k_part, v_part = later_part(far, start, t, block)
        acc[:, PAIR : 2 * PAIR] += k_part
        acc[:, 2 * PAIR : 3 * PAIR] += v_part


def final_body(done, rest_fars, start_ref, who, t, acc_in, *refs):
    refs = list(refs)
    columns = [refs.pop(0) for _ in range(ROW)]
    parts = [refs.pop(0) for _ in done]
    blocks = [refs.pop(0) for _ in rest_fars]
    acc, small, longest, count, rows, starts = refs
    shard = lax.axis_index("seq")
    start = start_ref[0]
    z = lax.rem(shard, ROW)
    for block, dz in zip(columns, range(ROW)):
        piece = block[TOK : TOK + 48, :].astype(F32)
        zz = lax.rem(z + dz, ROW)
        for x in range(COLS):
            at = x * ROW + zz
            rows[pl.ds(pl.multiple_of(at * 8, 8), 8), :] = piece[8 * x : 8 * x + 8, :]
            starts[pl.ds(at, 1), :] = piece[32 + 4 * x : 33 + 4 * x, :]
    begin = starts[...]
    sub = lax.broadcasted_iota(I32, (SHARDS, TOK), 0)
    lane = lax.broadcasted_iota(I32, (SHARDS, TOK), 1)
    along = jnp.sum(jnp.where(sub == lane, begin, 0.0), axis=0, keepdims=True)
    stops = (lane > sub) & (lane < SHARDS) & (along < TOK)
    last = jnp.min(jnp.where(stops, lane, SHARDS - 1).astype(F32), axis=1, keepdims=True)
    sub1 = lax.broadcasted_iota(I32, (SHARDS, 1), 0)
    longest[0] = jnp.max(last - sub1.astype(F32)).astype(I32)
    mine = jnp.sum(jnp.where(sub1 == shard, last, 0.0)).astype(I32)
    reach = mine - shard
    count[0] = reach
    owner = who[0:1, :]
    place = who[1:2, :]
    theirs = jnp.sum(jnp.where(sub == owner, begin, 0.0), axis=0, keepdims=True).astype(I32)
    here = owner == shard
    after = (owner > shard) & (owner <= mine) & (place < theirs)
    carry_lo = jnp.where(start == TOK, 0, start)
    lo = jnp.where(here, jnp.where(place >= start, start, 0), carry_lo)
    hi = jnp.where(here, place, jnp.where(after, TOK - 1, -1))
    both = rows[...].astype(BF16)
    k, v = t[:, 2 * PAIR : 3 * PAIR], t[:, 3 * PAIR : 4 * PAIR]
    _, k_part, v_part = attend(both[:, 0:PAIR], both[:, PAIR:], k, v, lo, hi)
    acc[:, 0:PAIR] = acc_in[:, 0:PAIR]
    acc[:, PAIR : 2 * PAIR] = acc_in[:, PAIR : 2 * PAIR] + k_part
    acc[:, 2 * PAIR : 3 * PAIR] = acc_in[:, 2 * PAIR : 3 * PAIR] + v_part
    for fars, part in zip(done, parts):
        for n, far in enumerate(fars):

            @pl.when(far <= reach)
            def _():
                acc[:, PAIR : 3 * PAIR] += part[n]

    for far, block in zip(rest_fars, blocks):
        add_later(far, reach, start, t, block, acc)
    small[...] = acc[...].astype(BF16)


def further_body(start_ref, count, base, t, acc_in, *rest):
    blocks, acc = rest[:-1], rest[-1]
    acc[...] = acc_in[...]
    for n, block in enumerate(blocks):
        add_later(base[0] + n + 1, count[0], start_ref[0], t, block, acc)


ACC = jax.ShapeDtypeStruct((TOK, 3 * PAIR), F32)
BLOCK = jax.ShapeDtypeStruct((TOK + 48, 2 * PAIR), BF16)
BLOCK_FLOPS = 8 * 2 * TOK * TOK * PAIR


def later_call(fars, start, t, blocks):
    return call(
        functools.partial(later_body, fars),
        jax.ShapeDtypeStruct((len(fars), TOK, 2 * PAIR), F32),
        [SMEM] + [VMEM] * (1 + len(fars)), VMEM, BLOCK_FLOPS * len(fars), name="later",
    )(start, t, *blocks)


def further_call(start, count, base, t, acc, blocks):
    return call(
        further_body, ACC, [SMEM, SMEM, SMEM] + [VMEM] * (2 + len(blocks)), VMEM,
        BLOCK_FLOPS * len(blocks), aliases={4: 0}, name="further",
    )(start, count, base, t, acc, *blocks)


def shift(x, d):
    return lax.ppermute(x, "seq", [((i + d) % SHARDS, i) for i in range(SHARDS)])


def body(
    queries, keys, values, out_grad, prefix_state, variant_queries, variant_grads,
    variant_owner, variant_position, start,
):
    heads = queries.shape[1] // PAIR
    rows = queries.shape[0]
    anywhere = pl.BlockSpec(memory_space=pltpu.HBM)
    sent, msg = call(
        pack_body,
        (
            jax.ShapeDtypeStruct((heads, rows, 4 * PAIR), BF16),
            jax.ShapeDtypeStruct((16, 2 * PAIR), BF16),
        ),
        [SMEM] + [anywhere] * 4 + [VMEM] * 2, (VMEM, VMEM), 1 << 20,
        scratch=(pltpu.VMEM((4, rows, heads * PAIR), BF16), pltpu.SemaphoreType.DMA((4,))),
        name="pack", vmem=60,
    )(start, queries, out_grad, keys, values, variant_queries, variant_grads)
    msgs = [msg] + [shift(msg, ROW * d) for d in range(1, COLS)]
    t = lax.all_to_all(sent, "heads", split_axis=0, concat_axis=0).reshape(TOK, 4 * PAIR)
    own = call(
        assemble_body, BLOCK, [VMEM] * (1 + COLS), VMEM, 1 << 20,
        scratch=(pltpu.VMEM((32, 2 * PAIR), F32),), name="assemble",
    )(t, *msgs)

    blocks = {far: shift(own, far) for far in (7, 2, 8, 1)}
    for far, via in ((5, 7), (6, 7), (4, 2), (3, 2)):
        blocks[far] = shift(blocks[via], far - via)
    acc, who = call(
        own_body, (ACC, jax.ShapeDtypeStruct((8, TOK), I32)), [SMEM, VMEM, VMEM, VMEM],
        (VMEM, VMEM), BLOCK_FLOPS * 3 // 2, name="own",
    )(start, variant_owner.reshape(1, TOK), variant_position.reshape(1, TOK), t)
    acc = call(
        state_body, ACC, [SMEM, VMEM, VMEM, VMEM], VMEM, 3 * BLOCK_FLOPS,
        scratch=(
            pltpu.VMEM((4, FEAT, PAIR), F32),
            pltpu.VMEM((4, HEAD, PAIR), F32),
            pltpu.VMEM((4, HEAD, PAIR), F32),
            pltpu.VMEM((4, HEAD, PAIR), F32),
        ),
        aliases={3: 0}, name="state",
    )(start, prefix_state[0], t, acc)
    near, second, acc = lax.optimization_barrier((blocks[1], blocks[2], acc))
    blocks[9], blocks[10] = shift(near, ROW), shift(second, ROW)
    done = ((1, 8), (2, 7), (4, 5))
    parts = [later_call(fars, start, t, [blocks[far] for far in fars]) for fars in done]
    left = (3, 6, 9, 10)
    one = jax.ShapeDtypeStruct((1,), I32)
    columns = [own] + [blocks[far] for far in range(1, ROW)]
    acc, small, longest, count = call(
        functools.partial(final_body, done, left),
        (ACC, jax.ShapeDtypeStruct(ACC.shape, BF16), one, one),
        [SMEM] + [VMEM] * (3 + ROW + len(done) + len(left)), (VMEM, VMEM, SMEM, SMEM),
        BLOCK_FLOPS,
        scratch=(pltpu.VMEM((TOK, 2 * PAIR), F32), pltpu.VMEM((SHARDS, 2 * PAIR), F32)),
        aliases={3: 0}, name="final",
    )(
        start, who, t, acc,
        *columns, *parts, *[blocks[far] for far in left],
    )
    longest = longest.reshape(())

    def extend(acc, small):
        def go(carry):
            return carry[0] < longest

        def more(carry):
            base, near, far, acc = carry
            moved = [shift(block, ROW) for block in near]
            acc = further_call(start, count, base.reshape(1), t, acc, moved)
            return base + len(near), far, moved, acc

        near = [blocks[n] for n in (3, 4, 5, 6)]
        far = [blocks[n] for n in (7, 8, 9, 10)]
        return lax.while_loop(go, more, (jnp.int32(REACH), near, far, acc))[3].astype(BF16)

    small = lax.cond(longest > REACH, extend, lambda acc, small: small, acc, small)
    back = lax.all_to_all(small.reshape(heads, rows, 3 * PAIR), "heads", split_axis=0, concat_axis=0)
    out = jax.ShapeDtypeStruct((rows, heads * PAIR), F32)
    return tuple(call(unpack_body, (out, out, out), [VMEM], (VMEM,) * 3, 1 << 20, name="unpack")(back))


def solution(mesh):
    tokens = P(("seq", "heads"), None)
    in_specs = (
        tokens, tokens, tokens, tokens, P("seq", None, "heads"), P("seq", "heads"),
        P("seq", "heads"), P(), P(), P("seq"),
    )
    return jax.shard_map(
        body, mesh=mesh, in_specs=in_specs, out_specs=(tokens,) * 3, check_vma=False
    )
```

profile of v0, /device:TPU:1, one launch (start us, length us, event | category | flops | bytes accessed | tf_op | source)
XLA Modules:
  0.0 66.2 jit_solution(11617895090137245033)
XLA Ops:
  1.3 2.4 %pack.1 = (bf16[8,32,512]{2,1,0:T(8,128)(2,1)}, bf16[16,256]{1,0:T(8,128)(2,1)}) custom-call(s32[1]{0:T(128)S(6)} %copy.52.start.start_ref, bf16[32,1024]{1,0:T(8,128)(2,1)} %q.1, bf16[32,1024]{1,0:T(8,128)(2,1)} %g.1, bf16[32,1024]{1,0:T(8,128)(2,1)} %k.1, bf16[32,1024]{1,0:T(8,128)(2,1)} %v.1, bf16[8,128]{1,0:T(8,128)(2,1)} %vq.1, bf16[8,128]{1,0:T(8,128)(2,1)} %vg.1), custom_call_target="tpu_custom_call" | custom-call | flops 1048576 | bytes 1048576 | tf_op jit(solution)/shard_map/pack/pallas_call | solution.py:291
  3.7 0.0 copy-start.1
  3.7 0.0 copy-start.2
  3.7 0.0 copy-start.3
  3.7 6.7 %all-to-all-start = ((bf16[8,32,512]{2,1,0:T(8,128)(2,1)}), bf16[8,32,512]{2,1,0:T(8,128)(2,1)S(1)}, u32[]{:S(2)}, u32[]{:S(2)}) async-start(bf16[8,32,512]{2,1,0:T(8,128)(2,1)} %get-tuple-element.130), calls=%async_computation | async-start | bytes 524288 | tf_op jit(solution)/shard_map/all_to_all | solution.py:302
  10.4 0.0 copy-done.1
  10.4 0.6 collective-permute-start.6
  11.1 2.5 %collective-permute-start.5 = (bf16[16,256]{1,0:T(8,128)(2,1)S(1)}, bf16[16,256]{1,0:T(8,128)(2,1)S(1)}, u32[]{:S(2)}, u32[]{:S(2)}) collective-permute-start(bf16[16,256]{1,0:T(8,128)(2,1)S(1)} %copy-done.1), channel_id=1, source_target_pairs={{16,0},{17,1},{18,2},{19,3},{20,4},{21,5},{22,6},{23,7},{24,8},{25... | collective-permute-start | bytes 24584 | tf_op jit(solution)/shard_map/ppermute | solution.py:281
  13.5 1.2 %collective-permute-start.4 = (bf16[16,256]{1,0:T(8,128)(2,1)S(1)}, bf16[16,256]{1,0:T(8,128)(2,1)S(1)}, u32[]{:S(2)}, u32[]{:S(2)}) collective-permute-start(bf16[16,256]{1,0:T(8,128)(2,1)S(1)} %copy-done.1), channel_id=1, source_target_pairs={{8,0},{9,1},{10,2},{11,3},{12,4},{13,5},{14,6},{15,7},{16,8},{17,9... | collective-permute-start | bytes 24584 | tf_op jit(solution)/shard_map/ppermute | solution.py:281
  14.7 0.0 collective-permute-done.6.rest_3_
  14.7 0.5 collective-permute-done.5.rest_2_
  15.1 1.1 %collective-permute-done.4.rest_1_ = bf16[16,256]{1,0:T(8,128)(2,1)S(1)} collective-permute-done((bf16[16,256]{1,0:T(8,128)(2,1)S(1)}, bf16[16,256]{1,0:T(8,128)(2,1)S(1)}, u32[]{:S(2)}, u32[]{:S(2)}) %collective-permute-start.4) | collective-permute-done | bytes 8224 | tf_op jit(solution)/shard_map/ppermute | solution.py:281
  16.3 0.7 %all-to-all-done = bf16[8,32,512]{2,1,0:T(8,128)(2,1)S(1)} async-done(((bf16[8,32,512]{2,1,0:T(8,128)(2,1)}), bf16[8,32,512]{2,1,0:T(8,128)(2,1)S(1)}, u32[]{:S(2)}, u32[]{:S(2)}) %all-to-all-start) | async-done | bytes 262176 | tf_op jit(solution)/shard_map/all_to_all | solution.py:302
  16.9 0.0 copy-start
  17.0 3.3 %collective-permute-start.11 = (bf16[304,256]{1,0:T(8,128)(2,1)S(1)}, bf16[304,256]{1,0:T(8,128)(2,1)S(1)}, u32[]{:S(2)}, u32[]{:S(2)}) collective-permute-start(bf16[304,256]{1,0:T(8,128)(2,1)S(1)} %assemble.1.refs_0_), channel_id=1, source_target_pairs={{7,0},{8,1},{9,2},{10,3},{11,4},{12,5},{13,6},{14,7},{15,8},{16,9}... | collective-permute-start | bytes 466952 | tf_op jit(solution)/shard_map/ppermute | solution.py:281
  20.3 5.4 %collective-permute-start.8 = (bf16[304,256]{1,0:T(8,128)(2,1)S(1)}, bf16[304,256]{1,0:T(8,128)(2,1)S(1)}, u32[]{:S(2)}, u32[]{:S(2)}) collective-permute-start(bf16[304,256]{1,0:T(8,128)(2,1)S(1)} %assemble.1.refs_0_), channel_id=1, source_target_pairs={{2,0},{3,1},{4,2},{5,3},{6,4},{7,5},{8,6},{9,7},{10,8},{11,9},{12,... | collective-permute-start | bytes 466952 | tf_op jit(solution)/shard_map/ppermute | solution.py:281
  25.7 0.7 %collective-permute-start.7 = (bf16[304,256]{1,0:T(8,128)(2,1)S(1)}, bf16[304,256]{1,0:T(8,128)(2,1)S(1)}, u32[]{:S(2)}, u32[]{:S(2)}) collective-permute-start(bf16[304,256]{1,0:T(8,128)(2,1)S(1)} %assemble.1.refs_0_), channel_id=1, source_target_pairs={{1,0},{2,1},{3,2},{4,3},{5,4},{6,5},{7,6},{8,7},{9,8},{10,9},{11,1... | collective-permute-start | bytes 466952 | tf_op jit(solution)/shard_map/ppermute | solution.py:281
  26.4 0.3 collective-permute-start.14
  26.7 0.0 collective-permute-done.11.rest_1_.refs_7_
  26.7 0.6 collective-permute-start.12
  27.2 0.0 copy-done.2
  27.2 0.0 copy-done.3
  27.2 0.6 own.1
  27.8 4.2 %collective-permute-done.8.rest_0_.refs_2_ = bf16[304,256]{1,0:T(8,128)(2,1)S(1)} collective-permute-done((bf16[304,256]{1,0:T(8,128)(2,1)S(1)}, bf16[304,256]{1,0:T(8,128)(2,1)S(1)}, u32[]{:S(2)}, u32[]{:S(2)}) %collective-permute-start.8) | collective-permute-done | bytes 155680 | tf_op jit(solution)/shard_map/ppermute | solution.py:281
  32.0 6.6 %collective-permute-start.10 = (bf16[304,256]{1,0:T(8,128)(2,1)S(1)}, bf16[304,256]{1,0:T(8,128)(2,1)S(1)}, u32[]{:S(2)}, u32[]{:S(2)}) collective-permute-start(bf16[304,256]{1,0:T(8,128)(2,1)S(1)} %collective-permute-done.8.rest_0_.refs_2_), channel_id=1, source_target_pairs={{2,0},{3,1},{4,2},{5,3},{6,4},{7,5},{8,6},{9,7},{10,8},{11,9},{12,... | collective-permute-start | bytes 466952 | tf_op jit(solution)/shard_map/ppermute | solution.py:281
  38.6 0.0 copy-done
  38.6 1.7 %state.1.acc_in = f32[256,384]{1,0:T(8,128)S(1)} custom-call(s32[1]{0:T(128)S(6)} %copy.52.start.start_ref, bf16[2080,128]{1,0:T(8,128)(2,1)S(1)} %bitcast.9, bf16[256,512]{1,0:T(8,128)(2,1)S(1)} %bitcast.14, f32[256,384]{1,0:T(8,128)S(1)} %get-tuple-element.133.acc_in), custom_call_target="tpu_custom_call", output_to_operand_aliasing={{}: (3, {})} | custom-call | flops 402653184 | bytes 1048576 | tf_op jit(solution)/shard_map/state/pallas_call | solution.py:315
  40.3 0.0 collective-permute-done.7.rest_0_.refs_1_
  40.3 0.1 collective-permute-start.15
  40.4 0.1 collective-permute-start.13
  40.5 0.0 collective-permute-done.14.rest_1_
  40.5 4.8 %collective-permute-start.9 = (bf16[304,256]{1,0:T(8,128)(2,1)S(1)}, bf16[304,256]{1,0:T(8,128)(2,1)S(1)}, u32[]{:S(2)}, u32[]{:S(2)}) collective-permute-start(bf16[304,256]{1,0:T(8,128)(2,1)S(1)} %collective-permute-done.8.rest_0_.refs_2_), channel_id=1, source_target_pairs={{1,0},{2,1},{3,2},{4,3},{5,4},{6,5},{7,6},{8,7},{9,8},{10,9},{11,1... | collective-permute-start | bytes 466952 | tf_op jit(solution)/shard_map/ppermute | solution.py:281
  45.3 0.0 collective-permute-done.12.rest_1_.refs_5_
  45.3 0.0 collective-permute-start.16
  45.3 0.9 %later.4.refs_9_ = f32[2,256,256]{2,1,0:T(8,128)S(1)} custom-call(s32[1]{0:T(128)S(6)} %copy.52.start.start_ref, bf16[256,512]{1,0:T(8,128)(2,1)S(1)} %bitcast.15, bf16[304,256]{1,0:T(8,128)(2,1)S(1)} %collective-permute-done.8.rest_0_.refs_2_, bf16[304,256]{1,0:T(8,128)(2,1)S(1)} %collective-permute-done.11.rest_1_.refs_7_), custom_call_target="tpu_custom_call" | custom-call | flops 268435456 | bytes 1048576 | tf_op jit(solution)/shard_map/later/pallas_call | solution.py:266
  46.2 0.9 %later.3.refs_8_ = f32[2,256,256]{2,1,0:T(8,128)S(1)} custom-call(s32[1]{0:T(128)S(6)} %copy.52.start.start_ref, bf16[256,512]{1,0:T(8,128)(2,1)S(1)} %bitcast.16, bf16[304,256]{1,0:T(8,128)(2,1)S(1)} %collective-permute-done.7.rest_0_.refs_1_, bf16[304,256]{1,0:T(8,128)(2,1)S(1)} %collective-permute-done.14.rest_1_), custom_call_target="tpu_custom_call" | custom-call | flops 268435456 | bytes 1048576 | tf_op jit(solution)/shard_map/later/pallas_call | solution.py:266
  47.0 0.0 collective-permute-done.10.rest_0_.refs_4_
  47.0 0.8 %later.5.refs_10_ = f32[2,256,256]{2,1,0:T(8,128)S(1)} custom-call(s32[1]{0:T(128)S(6)} %copy.52.start.start_ref, bf16[256,512]{1,0:T(8,128)(2,1)S(1)} %bitcast.17, bf16[304,256]{1,0:T(8,128)(2,1)S(1)} %collective-permute-done.10.rest_0_.refs_4_, bf16[304,256]{1,0:T(8,128)(2,1)S(1)} %collective-permute-done.12.rest_1_.refs_5_), custom_call_target="tpu_custom_call" | custom-call | flops 268435456 | bytes 1048576 | tf_op jit(solution)/shard_map/later/pallas_call | solution.py:266
  47.9 0.0 collective-permute-done.13.refs_6_.refs_12_
  47.9 0.0 collective-permute-done.9.refs_3_.refs_11_
  47.9 0.0 collective-permute-done.15.refs_13_
  47.9 1.8 %collective-permute-done.16.refs_14_ = bf16[304,256]{1,0:T(8,128)(2,1)S(1)} collective-permute-done((bf16[304,256]{1,0:T(8,128)(2,1)S(1)}, bf16[304,256]{1,0:T(8,128)(2,1)S(1)}, u32[]{:S(2)}, u32[]{:S(2)}) %collective-permute-start.16) | collective-permute-done | bytes 155680 | tf_op jit(solution)/shard_map/ppermute | solution.py:281
  49.7 2.5 %final.1 = (f32[256,384]{1,0:T(8,128)S(1)}, bf16[256,384]{1,0:T(8,128)(2,1)S(1)}, s32[1]{0:T(128)}, s32[1]{0:T(128)}) custom-call(s32[1]{0:T(128)S(6)} %copy.52.start.start_ref, s32[8,256]{1,0:T(8,128)S(1)} %get-tuple-element.131.who, bf16[256,512]{1,0:T(8,128)(2,1)S(1)} %bitcast.18, f32[256,384]{1,0:T(8,128)S(1)} %state.1.acc_in, ...), custom_call_target="tpu_custom_call", output_to_operand_aliasing={{0}: (3, {})} | custom-call | flops 134217728 | bytes 1048576 | tf_op jit(solution)/shard_map/final/pallas_call | solution.py:332
  52.8 12.6 %all_to_all.10.x = bf16[8,32,384]{2,1,0:T(8,128)(2,1)S(1)} all-to-all(bf16[8,32,384]{2,1,0:T(8,128)(2,1)S(1)} %bitcast.20), channel_id=1, replica_groups=mesh['heads'=8,'seq'=32] {'heads'}, dimensions={0} | all-to-all | bytes 393216 | tf_op jit(solution)/shard_map/all_to_all | solution.py:360
  65.4 0.8 %unpack.1 = (f32[32,1024]{1,0:T(8,128)}, f32[32,1024]{1,0:T(8,128)}, f32[32,1024]{1,0:T(8,128)}) custom-call(bf16[8,32,384]{2,1,0:T(8,128)(2,1)S(1)} %all_to_all.10.x), custom_call_target="tpu_custom_call" | custom-call | flops 1048576 | bytes 1048576 | tf_op jit(solution)/shard_map/unpack/pallas_call | solution.py:362
  (2 shorter events, 0.0 us)
Async XLA Ops:
  3.7 6.7 %copy-start.1 = (bf16[16,256]{1,0:T(8,128)(2,1)S(1)}, bf16[16,256]{1,0:T(8,128)(2,1)}, u32[]{:S(2)}) copy-start(bf16[16,256]{1,0:T(8,128)(2,1)} %get-tuple-element.132.rest_0_) | copy-start | bytes 24580
  3.7 23.5 %copy-start.2 = (s32[256]{0:T(256)S(1)}, s32[256]{0:T(256)}, u32[]{:S(2)}) copy-start(s32[256]{0:T(256)} %param.21) | copy-start | bytes 3076
  3.7 23.5 %copy-start.3 = (s32[256]{0:T(256)S(1)}, s32[256]{0:T(256)}, u32[]{:S(2)}) copy-start(s32[256]{0:T(256)} %param.22) | copy-start | bytes 3076
  3.7 13.2 %all-to-all-start = ((bf16[8,32,512]{2,1,0:T(8,128)(2,1)}), bf16[8,32,512]{2,1,0:T(8,128)(2,1)S(1)}, u32[]{:S(2)}, u32[]{:S(2)}) async-start(bf16[8,32,512]{2,1,0:T(8,128)(2,1)} %get-tuple-element.130), calls=%async_computation | async-start | bytes 524288 | tf_op jit(solution)/shard_map/all_to_all | solution.py:302
  10.4 4.3 %collective-permute-start.6 = (bf16[16,256]{1,0:T(8,128)(2,1)S(1)}, bf16[16,256]{1,0:T(8,128)(2,1)S(1)}, u32[]{:S(2)}, u32[]{:S(2)}) collective-permute-start(bf16[16,256]{1,0:T(8,128)(2,1)S(1)} %copy-done.1), channel_id=1, source_target_pairs={{24,0},{25,1},{26,2},{27,3},{28,4},{29,5},{30,6},{31,7},{0,8},{1,9... | collective-permute-start | bytes 24584 | tf_op jit(solution)/shard_map/ppermute | solution.py:281
  11.1 4.1 %collective-permute-start.5 = (bf16[16,256]{1,0:T(8,128)(2,1)S(1)}, bf16[16,256]{1,0:T(8,128)(2,1)S(1)}, u32[]{:S(2)}, u32[]{:S(2)}) collective-permute-start(bf16[16,256]{1,0:T(8,128)(2,1)S(1)} %copy-done.1), channel_id=1, source_target_pairs={{16,0},{17,1},{18,2},{19,3},{20,4},{21,5},{22,6},{23,7},{24,8},{25... | collective-permute-start | bytes 24584 | tf_op jit(solution)/shard_map/ppermute | solution.py:281
  13.5 2.7 %collective-permute-start.4 = (bf16[16,256]{1,0:T(8,128)(2,1)S(1)}, bf16[16,256]{1,0:T(8,128)(2,1)S(1)}, u32[]{:S(2)}, u32[]{:S(2)}) collective-permute-start(bf16[16,256]{1,0:T(8,128)(2,1)S(1)} %copy-done.1), channel_id=1, source_target_pairs={{8,0},{9,1},{10,2},{11,3},{12,4},{13,5},{14,6},{15,7},{16,8},{17,9... | collective-permute-start | bytes 24584 | tf_op jit(solution)/shard_map/ppermute | solution.py:281
  16.9 21.7 %copy-start = (bf16[1,2080,128]{2,1,0:T(8,128)(2,1)S(1)}, bf16[1,2080,128]{2,1,0:T(8,128)(2,1)}, u32[]{:S(2)}) copy-start(bf16[1,2080,128]{2,1,0:T(8,128)(2,1)} %param.18) | copy-start | bytes 1597444
  17.0 9.7 %collective-permute-start.11 = (bf16[304,256]{1,0:T(8,128)(2,1)S(1)}, bf16[304,256]{1,0:T(8,128)(2,1)S(1)}, u32[]{:S(2)}, u32[]{:S(2)}) collective-permute-start(bf16[304,256]{1,0:T(8,128)(2,1)S(1)} %assemble.1.refs_0_), channel_id=1, source_target_pairs={{7,0},{8,1},{9,2},{10,3},{11,4},{12,5},{13,6},{14,7},{15,8},{16,9}... | collective-permute-start | bytes 466952 | tf_op jit(solution)/shard_map/ppermute | solution.py:281
  20.3 11.8 %collective-permute-start.8 = (bf16[304,256]{1,0:T(8,128)(2,1)S(1)}, bf16[304,256]{1,0:T(8,128)(2,1)S(1)}, u32[]{:S(2)}, u32[]{:S(2)}) collective-permute-start(bf16[304,256]{1,0:T(8,128)(2,1)S(1)} %assemble.1.refs_0_), channel_id=1, source_target_pairs={{2,0},{3,1},{4,2},{5,3},{6,4},{7,5},{8,6},{9,7},{10,8},{11,9},{12,... | collective-permute-start | bytes 466952 | tf_op jit(solution)/shard_map/ppermute | solution.py:281
  25.7 14.7 %collective-permute-start.7 = (bf16[304,256]{1,0:T(8,128)(2,1)S(1)}, bf16[304,256]{1,0:T(8,128)(2,1)S(1)}, u32[]{:S(2)}, u32[]{:S(2)}) collective-permute-start(bf16[304,256]{1,0:T(8,128)(2,1)S(1)} %assemble.1.refs_0_), channel_id=1, source_target_pairs={{1,0},{2,1},{3,2},{4,3},{5,4},{6,5},{7,6},{8,7},{9,8},{10,9},{11,1... | collective-permute-start | bytes 466952 | tf_op jit(solution)/shard_map/ppermute | solution.py:281
  26.4 14.1 %collective-permute-start.14 = (bf16[304,256]{1,0:T(8,128)(2,1)S(1)}, bf16[304,256]{1,0:T(8,128)(2,1)S(1)}, u32[]{:S(2)}, u32[]{:S(2)}) collective-permute-start(bf16[304,256]{1,0:T(8,128)(2,1)S(1)} %assemble.1.refs_0_), channel_id=1, source_target_pairs={{8,0},{9,1},{10,2},{11,3},{12,4},{13,5},{14,6},{15,7},{16,8},{17,9... | collective-permute-start | bytes 466952 | tf_op jit(solution)/shard_map/ppermute | solution.py:281
  26.7 18.6 %collective-permute-start.12 = (bf16[304,256]{1,0:T(8,128)(2,1)S(1)}, bf16[304,256]{1,0:T(8,128)(2,1)S(1)}, u32[]{:S(2)}, u32[]{:S(2)}) collective-permute-start(bf16[304,256]{1,0:T(8,128)(2,1)S(1)} %collective-permute-done.11.rest_1_.refs_7_), channel_id=1, source_target_pairs={{30,0},{31,1},{0,2},{1,3},{2,4},{3,5},{4,6},{5,7},{6,8},{7,9},{8,1... | collective-permute-start | bytes 466952 | tf_op jit(solution)/shard_map/ppermute | solution.py:281
  32.0 15.0 %collective-permute-start.10 = (bf16[304,256]{1,0:T(8,128)(2,1)S(1)}, bf16[304,256]{1,0:T(8,128)(2,1)S(1)}, u32[]{:S(2)}, u32[]{:S(2)}) collective-permute-start(bf16[304,256]{1,0:T(8,128)(2,1)S(1)} %collective-permute-done.8.rest_0_.refs_2_), channel_id=1, source_target_pairs={{2,0},{3,1},{4,2},{5,3},{6,4},{7,5},{8,6},{9,7},{10,8},{11,9},{12,... | collective-permute-start | bytes 466952 | tf_op jit(solution)/shard_map/ppermute | solution.py:281
  40.3 7.6 %collective-permute-start.15 = (bf16[304,256]{1,0:T(8,128)(2,1)S(1)}, bf16[304,256]{1,0:T(8,128)(2,1)S(1)}, u32[]{:S(2)}, u32[]{:S(2)}) collective-permute-start(bf16[304,256]{1,0:T(8,128)(2,1)S(1)} %collective-permute-done.7.rest_0_.refs_1_), channel_id=1, source_target_pairs={{8,0},{9,1},{10,2},{11,3},{12,4},{13,5},{14,6},{15,7},{16,8},{17,9... | collective-permute-start | bytes 466952 | tf_op jit(solution)/shard_map/ppermute | solution.py:281
  40.4 7.5 %collective-permute-start.13 = (bf16[304,256]{1,0:T(8,128)(2,1)S(1)}, bf16[304,256]{1,0:T(8,128)(2,1)S(1)}, u32[]{:S(2)}, u32[]{:S(2)}) collective-permute-start(bf16[304,256]{1,0:T(8,128)(2,1)S(1)} %collective-permute-done.11.rest_1_.refs_7_), channel_id=1, source_target_pairs={{31,0},{0,1},{1,2},{2,3},{3,4},{4,5},{5,6},{6,7},{7,8},{8,9},{9,10... | collective-permute-start | bytes 466952 | tf_op jit(solution)/shard_map/ppermute | solution.py:281
  40.5 7.4 %collective-permute-start.9 = (bf16[304,256]{1,0:T(8,128)(2,1)S(1)}, bf16[304,256]{1,0:T(8,128)(2,1)S(1)}, u32[]{:S(2)}, u32[]{:S(2)}) collective-permute-start(bf16[304,256]{1,0:T(8,128)(2,1)S(1)} %collective-permute-done.8.rest_0_.refs_2_), channel_id=1, source_target_pairs={{1,0},{2,1},{3,2},{4,3},{5,4},{6,5},{7,6},{8,7},{9,8},{10,9},{11,1... | collective-permute-start | bytes 466952 | tf_op jit(solution)/shard_map/ppermute | solution.py:281
  45.3 4.4 %collective-permute-start.16 = (bf16[304,256]{1,0:T(8,128)(2,1)S(1)}, bf16[304,256]{1,0:T(8,128)(2,1)S(1)}, u32[]{:S(2)}, u32[]{:S(2)}) collective-permute-start(bf16[304,256]{1,0:T(8,128)(2,1)S(1)} %collective-permute-done.8.rest_0_.refs_2_), channel_id=1, source_target_pairs={{8,0},{9,1},{10,2},{11,3},{12,4},{13,5},{14,6},{15,7},{16,8},{17,9... | collective-permute-start | bytes 466952 | tf_op jit(solution)/shard_map/ppermute | solution.py:281
where the time goes:
time: 65.9 us; the launch traced here: 66.2 us
  starting transfers between devices  32.7 us (50%)
  blocking collectives  12.6 us (19%)
  Pallas kernels  10.5 us (16%)
  waiting for transfers between devices  8.29 us (13%)
  between operations  2.07 us (3%)
    ppermute x13, starting transfers between devices, shift(): lax.ppermute(x, 'seq', [((i + d) % SHARDS, i) for i in range(SHARDS)])  26 us
    all_to_all x1, blocking collectives, body(): lax.all_to_all(small.reshape(heads, rows, 3 * PAIR), 'heads', split_axis=...  12.6 us
    ppermute x13, waiting for transfers between devices, shift(): lax.ppermute(x, 'seq', [((i + d) % SHARDS, i) for i in range(SHARDS)])  7.61 us
    all_to_all x1, starting transfers between devices, body(): lax.all_to_all(sent, 'heads', split_axis=0, concat_axis=0)  6.7 us
    pallas_call x3, Pallas kernels, later_call(): call(functools.partial(later_body, fars), jax.ShapeDtypeStruct((len(fars)...  2.56 us
    pallas_call x1, Pallas kernels, body(): call(functools.partial(final_body, done, left), (ACC, jax.ShapeDtypeStruc...  2.45 us
    pallas_call x1, Pallas kernels, body(): call(pack_body, (jax.ShapeDtypeStruct((heads, rows, 4 * PAIR), BF16), jax...  2.4 us
    pallas_call x1, Pallas kernels, body(): call(state_body, ACC, [SMEM, VMEM, VMEM, VMEM], VMEM, 3 * BLOCK_FLOPS, sc...  1.72 us
  transfers between devices with their start and end apart: 14, of which 5 were waited for; matrix products, arithmetic and copies ran while one was open for 0% of the time, Pallas kernels for 7%

commit v1 on v0

--- a/solution.py
+++ b/solution.py
@@ -95,14 +95,14 @@
 
 
 def assemble_body(t, *rest):
-    msgs, (block, rows) = rest[:COLS], rest[COLS:]
+    msgs, (block, rows) = rest[:2], rest[2:]
     x = lax.div(lax.axis_index("seq"), ROW)
     block[0:TOK, :] = t[:, 0 : 2 * PAIR]
     group = lax.shift_right_logical(lax.broadcasted_iota(I32, (16, 2 * PAIR), 0), 2)
     starts = jnp.zeros((16, 2 * PAIR), F32)
-    for dx, msg in enumerate(msgs):
+    for dx in range(COLS):
         at = lax.rem(x + dx, COLS)
-        piece = msg[...].astype(F32)
+        piece = msgs[dx % 2][dx // 2 * 16 : dx // 2 * 16 + 16, :].astype(F32)
         rows[pl.ds(pl.multiple_of(at * 8, 8), 8), :] = piece[0:8, :]
         starts = jnp.where(group == at, piece[8:9, :], starts)
     block[TOK : TOK + 32, :] = rows[...].astype(BF16)
@@ -298,15 +298,16 @@
         scratch=(pltpu.VMEM((4, rows, heads * PAIR), BF16), pltpu.SemaphoreType.DMA((4,))),
         name="pack", vmem=60,
     )(start, queries, out_grad, keys, values, variant_queries, variant_grads)
-    msgs = [msg] + [shift(msg, ROW * d) for d in range(1, COLS)]
+    msgs = jnp.concatenate([msg, shift(msg, 2 * ROW)], 0)
+    msgs = (msgs, shift(msgs, ROW))
     t = lax.all_to_all(sent, "heads", split_axis=0, concat_axis=0).reshape(TOK, 4 * PAIR)
     own = call(
-        assemble_body, BLOCK, [VMEM] * (1 + COLS), VMEM, 1 << 20,
+        assemble_body, BLOCK, [VMEM] * 3, VMEM, 1 << 20,
         scratch=(pltpu.VMEM((32, 2 * PAIR), F32),), name="assemble",
     )(t, *msgs)
 
-    blocks = {far: shift(own, far) for far in (7, 2, 8, 1)}
-    for far, via in ((5, 7), (6, 7), (4, 2), (3, 2)):
+    blocks = {far: shift(own, far) for far in (8, 2, 1)}
+    for far, via in ((6, 8), (7, 8), (4, 2), (3, 2), (5, 6)):
         blocks[far] = shift(blocks[via], far - via)
     acc, who = call(
         own_body, (ACC, jax.ShapeDtypeStruct((8, TOK), I32)), [SMEM, VMEM, VMEM, VMEM],
@@ -322,11 +323,11 @@
         ),
         aliases={3: 0}, name="state",
     )(start, prefix_state[0], t, acc)
-    near, second, acc = lax.optimization_barrier((blocks[1], blocks[2], acc))
+    near, second, acc, _ = lax.optimization_barrier((blocks[1], blocks[2], acc, blocks[6]))
     blocks[9], blocks[10] = shift(near, ROW), shift(second, ROW)
-    done = ((1, 8), (2, 7), (4, 5))
+    done = ((1, 8), (2, 7), (4, 6))
     parts = [later_call(fars, start, t, [blocks[far] for far in fars]) for fars in done]
-    left = (3, 6, 9, 10)
+    left = (3, 5, 9, 10)
     one = jax.ShapeDtypeStruct((1,), I32)
     columns = [own] + [blocks[far] for far in range(1, ROW)]
     acc, small, longest, count = call(

time: 65.9 us -> 72.5 us (1.10)
  blocking collectives: 12.6 us -> 18.9 us
    all_to_all x1, blocking collectives: 12.6 us -> 18.9 us  [body(): lax.all_to_all(small.reshape(heads, rows, 3 * PAIR), 'heads', split_axis=...]
    ppermute x13 -> x12, waiting for transfers between devices: 7.61 us -> 8.23 us  [shift(): lax.ppermute(x, 'seq', [((i + d) % SHARDS, i) for i in range(SHARDS)])]
    ppermute x13 -> x12, starting transfers between devices: 26 us -> 26.2 us  [shift(): lax.ppermute(x, 'seq', [((i + d) % SHARDS, i) for i in range(SHARDS)])]
  transfers between devices with their start and end apart: 14 -> 13, of which waited for: 5 -> 5; matrix products, arithmetic and copies ran while one was open for 0% -> 0% of each run, Pallas kernels for 7% -> 7%
where the time goes in v1:
time: 72.5 us; the launch traced here: 72.4 us
  starting transfers between devices  32.8 us (45%)
  blocking collectives  18.9 us (26%)
  Pallas kernels  10.5 us (14%)
  waiting for transfers between devices  8.23 us (11%)
  between operations  2.05 us (3%)
    ppermute x12, starting transfers between devices, shift(): lax.ppermute(x, 'seq', [((i + d) % SHARDS, i) for i in range(SHARDS)])  26.2 us
    all_to_all x1, blocking collectives, body(): lax.all_to_all(small.reshape(heads, rows, 3 * PAIR), 'heads', split_axis=...  18.9 us
    ppermute x12, waiting for transfers between devices, shift(): lax.ppermute(x, 'seq', [((i + d) % SHARDS, i) for i in range(SHARDS)])  8.23 us
    all_to_all x1, starting transfers between devices, body(): lax.all_to_all(sent, 'heads', split_axis=0, concat_axis=0)  6.56 us
    pallas_call x3, Pallas kernels, later_call(): call(functools.partial(later_body, fars), jax.ShapeDtypeStruct((len(fars)...  2.56 us
    pallas_call x1, Pallas kernels, body(): call(functools.partial(final_body, done, left), (ACC, jax.ShapeDtypeStruc...  2.46 us
    pallas_call x1, Pallas kernels, body(): call(pack_body, (jax.ShapeDtypeStruct((heads, rows, 4 * PAIR), BF16), jax...  2.38 us
    pallas_call x1, Pallas kernels, body(): call(state_body, ACC, [SMEM, VMEM, VMEM, VMEM], VMEM, 3 * BLOCK_FLOPS, sc...  1.72 us
  transfers between devices with their start and end apart: 13, of which 5 were waited for; matrix products, arithmetic and copies ran while one was open for 0% of the time, Pallas kernels for 7%

profile of v1, /device:TPU:1, one launch (start us, length us, event | category | flops | bytes accessed | tf_op | source)
XLA Modules:
  0.0 72.4 jit_solution(6366868070200954380)
XLA Ops:
  1.3 2.4 %pack.1 = (bf16[8,32,512]{2,1,0:T(8,128)(2,1)}, bf16[16,256]{1,0:T(8,128)(2,1)}) custom-call(s32[1]{0:T(128)S(6)} %copy.53.start.start_ref, bf16[32,1024]{1,0:T(8,128)(2,1)} %q.1, bf16[32,1024]{1,0:T(8,128)(2,1)} %g.1, bf16[32,1024]{1,0:T(8,128)(2,1)} %k.1, bf16[32,1024]{1,0:T(8,128)(2,1)} %v.1, bf16[8,128]{1,0:T(8,128)(2,1)} %vq.1, bf16[8,128]{1,0:T(8,128)(2,1)} %vg.1), custom_call_target="tpu_custom_call" | custom-call | flops 1048576 | bytes 1048576 | tf_op jit(solution)/shard_map/pack/pallas_call | solution.py:291
  3.7 0.0 copy-start.3
  3.7 6.6 %all-to-all-start = ((bf16[8,32,512]{2,1,0:T(8,128)(2,1)}), bf16[8,32,512]{2,1,0:T(8,128)(2,1)S(1)}, u32[]{:S(2)}, u32[]{:S(2)}) async-start(bf16[8,32,512]{2,1,0:T(8,128)(2,1)} %get-tuple-element.130), calls=%async_computation | async-start | bytes 524288 | tf_op jit(solution)/shard_map/all_to_all | solution.py:303
  10.2 0.0 copy-done.3
  10.2 2.2 %collective-permute-start.4 = (bf16[16,256]{1,0:T(8,128)(2,1)S(1)}, bf16[16,256]{1,0:T(8,128)(2,1)S(1)}, u32[]{:S(2)}, u32[]{:S(2)}) collective-permute-start(bf16[16,256]{1,0:T(8,128)(2,1)S(1)} %copy-done.3), channel_id=1, source_target_pairs={{16,0},{17,1},{18,2},{19,3},{20,4},{21,5},{22,6},{23,7},{24,8},{25... | collective-permute-start | bytes 24584 | tf_op jit(solution)/shard_map/ppermute | solution.py:281
  12.4 1.8 %collective-permute-done.4 = bf16[16,256]{1,0:T(8,128)(2,1)S(1)} collective-permute-done((bf16[16,256]{1,0:T(8,128)(2,1)S(1)}, bf16[16,256]{1,0:T(8,128)(2,1)S(1)}, u32[]{:S(2)}, u32[]{:S(2)}) %collective-permute-start.4) | collective-permute-done | bytes 8224 | tf_op jit(solution)/shard_map/ppermute | solution.py:281
  14.2 0.0 copy-start.1
  14.3 0.0 copy-start.2
  14.3 1.9 %collective-permute-start.5 = (bf16[32,256]{1,0:T(8,128)(2,1)S(1)}, bf16[32,256]{1,0:T(8,128)(2,1)S(1)}, u32[]{:S(2)}, u32[]{:S(2)}) collective-permute-start(bf16[32,256]{1,0:T(8,128)(2,1)S(1)} %constant_dynamic-update-slice_fusion.rest_0_), channel_id=1, source_target_pairs={{8,0},{9,1},{10,2},{11,3},{12,4},{13,5},{14,6},{15,7},{16,8},{17,9... | collective-permute-start | bytes 49160 | tf_op jit(solution)/shard_map/ppermute | solution.py:281
  16.2 1.0 %collective-permute-done.5.rest_1_ = bf16[32,256]{1,0:T(8,128)(2,1)S(1)} collective-permute-done((bf16[32,256]{1,0:T(8,128)(2,1)S(1)}, bf16[32,256]{1,0:T(8,128)(2,1)S(1)}, u32[]{:S(2)}, u32[]{:S(2)}) %collective-permute-start.5) | collective-permute-done | bytes 16416 | tf_op jit(solution)/shard_map/ppermute | solution.py:281
  17.1 0.0 all-to-all-done
  17.1 0.0 copy-start
  17.2 2.9 %collective-permute-start.8 = (bf16[304,256]{1,0:T(8,128)(2,1)S(1)}, bf16[304,256]{1,0:T(8,128)(2,1)S(1)}, u32[]{:S(2)}, u32[]{:S(2)}) collective-permute-start(bf16[304,256]{1,0:T(8,128)(2,1)S(1)} %assemble.1.refs_0_), channel_id=1, source_target_pairs={{8,0},{9,1},{10,2},{11,3},{12,4},{13,5},{14,6},{15,7},{16,8},{17,9... | collective-permute-start | bytes 466952 | tf_op jit(solution)/shard_map/ppermute | solution.py:281
  20.1 5.8 %collective-permute-start.7 = (bf16[304,256]{1,0:T(8,128)(2,1)S(1)}, bf16[304,256]{1,0:T(8,128)(2,1)S(1)}, u32[]{:S(2)}, u32[]{:S(2)}) collective-permute-start(bf16[304,256]{1,0:T(8,128)(2,1)S(1)} %assemble.1.refs_0_), channel_id=1, source_target_pairs={{2,0},{3,1},{4,2},{5,3},{6,4},{7,5},{8,6},{9,7},{10,8},{11,9},{12,... | collective-permute-start | bytes 466952 | tf_op jit(solution)/shard_map/ppermute | solution.py:281
  25.9 0.7 %collective-permute-start.6 = (bf16[304,256]{1,0:T(8,128)(2,1)S(1)}, bf16[304,256]{1,0:T(8,128)(2,1)S(1)}, u32[]{:S(2)}, u32[]{:S(2)}) collective-permute-start(bf16[304,256]{1,0:T(8,128)(2,1)S(1)} %assemble.1.refs_0_), channel_id=1, source_target_pairs={{1,0},{2,1},{3,2},{4,3},{5,4},{6,5},{7,6},{8,7},{9,8},{10,9},{11,1... | collective-permute-start | bytes 466952 | tf_op jit(solution)/shard_map/ppermute | solution.py:281
  26.6 0.0 collective-permute-done.8.rest_1_
  26.6 1.2 %collective-permute-start.9 = (bf16[304,256]{1,0:T(8,128)(2,1)S(1)}, bf16[304,256]{1,0:T(8,128)(2,1)S(1)}, u32[]{:S(2)}, u32[]{:S(2)}) collective-permute-start(bf16[304,256]{1,0:T(8,128)(2,1)S(1)} %collective-permute-done.8.rest_1_), channel_id=1, source_target_pairs={{30,0},{31,1},{0,2},{1,3},{2,4},{3,5},{4,6},{5,7},{6,8},{7,9},{8,1... | collective-permute-start | bytes 466952 | tf_op jit(solution)/shard_map/ppermute | solution.py:281
  27.8 0.3 collective-permute-done.7.rest_0_.refs_2_
  28.2 6.2 %collective-permute-start.11 = (bf16[304,256]{1,0:T(8,128)(2,1)S(1)}, bf16[304,256]{1,0:T(8,128)(2,1)S(1)}, u32[]{:S(2)}, u32[]{:S(2)}) collective-permute-start(bf16[304,256]{1,0:T(8,128)(2,1)S(1)} %collective-permute-done.7.rest_0_.refs_2_), channel_id=1, source_target_pairs={{2,0},{3,1},{4,2},{5,3},{6,4},{7,5},{8,6},{9,7},{10,8},{11,9},{12,... | collective-permute-start | bytes 466952 | tf_op jit(solution)/shard_map/ppermute | solution.py:281
  34.4 0.0 copy-done.1
  34.4 0.0 copy-done.2
  34.4 0.6 own.1
  35.0 2.6 %collective-permute-start.13 = (bf16[304,256]{1,0:T(8,128)(2,1)S(1)}, bf16[304,256]{1,0:T(8,128)(2,1)S(1)}, u32[]{:S(2)}, u32[]{:S(2)}) collective-permute-start(bf16[304,256]{1,0:T(8,128)(2,1)S(1)} %collective-permute-done.8.rest_1_), channel_id=1, source_target_pairs={{31,0},{0,1},{1,2},{2,3},{3,4},{4,5},{5,6},{6,7},{7,8},{8,9},{9,10... | collective-permute-start | bytes 466952 | tf_op jit(solution)/shard_map/ppermute | solution.py:281
  37.5 0.0 copy-done
  37.5 1.7 %state.1.acc_in = f32[256,384]{1,0:T(8,128)S(1)} custom-call(s32[1]{0:T(128)S(6)} %copy.53.start.start_ref, bf16[2080,128]{1,0:T(8,128)(2,1)S(1)} %bitcast.9, bf16[256,512]{1,0:T(8,128)(2,1)S(1)} %bitcast.14, f32[256,384]{1,0:T(8,128)S(1)} %get-tuple-element.133.acc_in), custom_call_target="tpu_custom_call", output_to_operand_aliasing={{}: (3, {})} | custom-call | flops 402653184 | bytes 1048576 | tf_op jit(solution)/shard_map/state/pallas_call | solution.py:316
  39.3 2.4 %collective-permute-start.10 = (bf16[304,256]{1,0:T(8,128)(2,1)S(1)}, bf16[304,256]{1,0:T(8,128)(2,1)S(1)}, u32[]{:S(2)}, u32[]{:S(2)}) collective-permute-start(bf16[304,256]{1,0:T(8,128)(2,1)S(1)} %collective-permute-done.7.rest_0_.refs_2_), channel_id=1, source_target_pairs={{1,0},{2,1},{3,2},{4,3},{5,4},{6,5},{7,6},{8,7},{9,8},{10,9},{11,1... | collective-permute-start | bytes 466952 | tf_op jit(solution)/shard_map/ppermute | solution.py:281
  41.6 0.0 collective-permute-done.6.rest_0_.refs_1_
  41.6 0.0 collective-permute-done.9.rest_1_.refs_6_
  41.6 0.0 collective-permute-start.14
  41.6 0.1 collective-permute-start.12
  41.7 0.0 collective-permute-done.11.rest_0_.refs_4_
  41.7 0.3 collective-permute-start.15
  42.0 0.9 %later.3.refs_8_ = f32[2,256,256]{2,1,0:T(8,128)S(1)} custom-call(s32[1]{0:T(128)S(6)} %copy.53.start.start_ref, bf16[256,512]{1,0:T(8,128)(2,1)S(1)} %bitcast.15, bf16[304,256]{1,0:T(8,128)(2,1)S(1)} %collective-permute-done.6.rest_0_.refs_1_, bf16[304,256]{1,0:T(8,128)(2,1)S(1)} %collective-permute-done.8.rest_1_), custom_call_target="tpu_custom_call" | custom-call | flops 268435456 | bytes 1048576 | tf_op jit(solution)/shard_map/later/pallas_call | solution.py:266
  42.9 0.9 %later.5.refs_10_ = f32[2,256,256]{2,1,0:T(8,128)S(1)} custom-call(s32[1]{0:T(128)S(6)} %copy.53.start.start_ref, bf16[256,512]{1,0:T(8,128)(2,1)S(1)} %bitcast.16, bf16[304,256]{1,0:T(8,128)(2,1)S(1)} %collective-permute-done.11.rest_0_.refs_4_, bf16[304,256]{1,0:T(8,128)(2,1)S(1)} %collective-permute-done.9.rest_1_.refs_6_), custom_call_target="tpu_custom_call" | custom-call | flops 268435456 | bytes 1048576 | tf_op jit(solution)/shard_map/later/pallas_call | solution.py:266
  43.7 0.0 collective-permute-done.13.rest_1_.refs_7_
  43.7 0.9 %later.4.refs_9_ = f32[2,256,256]{2,1,0:T(8,128)S(1)} custom-call(s32[1]{0:T(128)S(6)} %copy.53.start.start_ref, bf16[256,512]{1,0:T(8,128)(2,1)S(1)} %bitcast.17, bf16[304,256]{1,0:T(8,128)(2,1)S(1)} %collective-permute-done.7.rest_0_.refs_2_, bf16[304,256]{1,0:T(8,128)(2,1)S(1)} %collective-permute-done.13.rest_1_.refs_7_), custom_call_target="tpu_custom_call" | custom-call | flops 268435456 | bytes 1048576 | tf_op jit(solution)/shard_map/later/pallas_call | solution.py:266
  44.6 1.9 %collective-permute-done.10.refs_3_.refs_11_ = bf16[304,256]{1,0:T(8,128)(2,1)S(1)} collective-permute-done((bf16[304,256]{1,0:T(8,128)(2,1)S(1)}, bf16[304,256]{1,0:T(8,128)(2,1)S(1)}, u32[]{:S(2)}, u32[]{:S(2)}) %collective-permute-start.10) | collective-permute-done | bytes 155680 | tf_op jit(solution)/shard_map/ppermute | solution.py:281
  46.5 3.2 %collective-permute-done.12.refs_5_.refs_12_ = bf16[304,256]{1,0:T(8,128)(2,1)S(1)} collective-permute-done((bf16[304,256]{1,0:T(8,128)(2,1)S(1)}, bf16[304,256]{1,0:T(8,128)(2,1)S(1)}, u32[]{:S(2)}, u32[]{:S(2)}) %collective-permute-start.12) | collective-permute-done | bytes 155680 | tf_op jit(solution)/shard_map/ppermute | solution.py:281
  49.7 0.0 collective-permute-done.14.refs_13_
  49.7 0.0 collective-permute-done.15.refs_14_
  49.7 2.5 %final.1 = (f32[256,384]{1,0:T(8,128)S(1)}, bf16[256,384]{1,0:T(8,128)(2,1)S(1)}, s32[1]{0:T(128)}, s32[1]{0:T(128)}) custom-call(s32[1]{0:T(128)S(6)} %copy.53.start.start_ref, s32[8,256]{1,0:T(8,128)S(1)} %get-tuple-element.131.who, bf16[256,512]{1,0:T(8,128)(2,1)S(1)} %bitcast.18, f32[256,384]{1,0:T(8,128)S(1)} %state.1.acc_in, ...), custom_call_target="tpu_custom_call", output_to_operand_aliasing={{0}: (3, {})} | custom-call | flops 134217728 | bytes 1048576 | tf_op jit(solution)/shard_map/final/pallas_call | solution.py:333
  52.8 18.9 %all_to_all.10.x = bf16[8,32,384]{2,1,0:T(8,128)(2,1)S(1)} all-to-all(bf16[8,32,384]{2,1,0:T(8,128)(2,1)S(1)} %bitcast.20), channel_id=1, replica_groups=mesh['heads'=8,'seq'=32] {'heads'}, dimensions={0} | all-to-all | bytes 393216 | tf_op jit(solution)/shard_map/all_to_all | solution.py:361
  71.7 0.8 %unpack.1 = (f32[32,1024]{1,0:T(8,128)}, f32[32,1024]{1,0:T(8,128)}, f32[32,1024]{1,0:T(8,128)}) custom-call(bf16[8,32,384]{2,1,0:T(8,128)(2,1)S(1)} %all_to_all.10.x), custom_call_target="tpu_custom_call" | custom-call | flops 1048576 | bytes 1048576 | tf_op jit(solution)/shard_map/unpack/pallas_call | solution.py:363
  (4 shorter events, 0.0 us)
Async XLA Ops:
  3.7 6.6 %copy-start.3 = (bf16[16,256]{1,0:T(8,128)(2,1)S(1)}, bf16[16,256]{1,0:T(8,128)(2,1)}, u32[]{:S(2)}) copy-start(bf16[16,256]{1,0:T(8,128)(2,1)} %get-tuple-element.132) | copy-start | bytes 24580
  3.7 13.5 %all-to-all-start = ((bf16[8,32,512]{2,1,0:T(8,128)(2,1)}), bf16[8,32,512]{2,1,0:T(8,128)(2,1)S(1)}, u32[]{:S(2)}, u32[]{:S(2)}) async-start(bf16[8,32,512]{2,1,0:T(8,128)(2,1)} %get-tuple-element.130), calls=%async_computation | async-start | bytes 524288 | tf_op jit(solution)/shard_map/all_to_all | solution.py:303
  10.2 4.0 %collective-permute-start.4 = (bf16[16,256]{1,0:T(8,128)(2,1)S(1)}, bf16[16,256]{1,0:T(8,128)(2,1)S(1)}, u32[]{:S(2)}, u32[]{:S(2)}) collective-permute-start(bf16[16,256]{1,0:T(8,128)(2,1)S(1)} %copy-done.3), channel_id=1, source_target_pairs={{16,0},{17,1},{18,2},{19,3},{20,4},{21,5},{22,6},{23,7},{24,8},{25... | collective-permute-start | bytes 24584 | tf_op jit(solution)/shard_map/ppermute | solution.py:281
  14.2 20.1 %copy-start.1 = (s32[256]{0:T(256)S(1)}, s32[256]{0:T(256)}, u32[]{:S(2)}) copy-start(s32[256]{0:T(256)} %param.21) | copy-start | bytes 3076
  14.3 20.1 %copy-start.2 = (s32[256]{0:T(256)S(1)}, s32[256]{0:T(256)}, u32[]{:S(2)}) copy-start(s32[256]{0:T(256)} %param.22) | copy-start | bytes 3076
  14.3 2.9 %collective-permute-start.5 = (bf16[32,256]{1,0:T(8,128)(2,1)S(1)}, bf16[32,256]{1,0:T(8,128)(2,1)S(1)}, u32[]{:S(2)}, u32[]{:S(2)}) collective-permute-start(bf16[32,256]{1,0:T(8,128)(2,1)S(1)} %constant_dynamic-update-slice_fusion.rest_0_), channel_id=1, source_target_pairs={{8,0},{9,1},{10,2},{11,3},{12,4},{13,5},{14,6},{15,7},{16,8},{17,9... | collective-permute-start | bytes 49160 | tf_op jit(solution)/shard_map/ppermute | solution.py:281
  17.1 20.4 %copy-start = (bf16[1,2080,128]{2,1,0:T(8,128)(2,1)S(1)}, bf16[1,2080,128]{2,1,0:T(8,128)(2,1)}, u32[]{:S(2)}) copy-start(bf16[1,2080,128]{2,1,0:T(8,128)(2,1)} %param.18) | copy-start | bytes 1597444
  17.2 9.5 %collective-permute-start.8 = (bf16[304,256]{1,0:T(8,128)(2,1)S(1)}, bf16[304,256]{1,0:T(8,128)(2,1)S(1)}, u32[]{:S(2)}, u32[]{:S(2)}) collective-permute-start(bf16[304,256]{1,0:T(8,128)(2,1)S(1)} %assemble.1.refs_0_), channel_id=1, source_target_pairs={{8,0},{9,1},{10,2},{11,3},{12,4},{13,5},{14,6},{15,7},{16,8},{17,9... | collective-permute-start | bytes 466952 | tf_op jit(solution)/shard_map/ppermute | solution.py:281
  20.1 8.1 %collective-permute-start.7 = (bf16[304,256]{1,0:T(8,128)(2,1)S(1)}, bf16[304,256]{1,0:T(8,128)(2,1)S(1)}, u32[]{:S(2)}, u32[]{:S(2)}) collective-permute-start(bf16[304,256]{1,0:T(8,128)(2,1)S(1)} %assemble.1.refs_0_), channel_id=1, source_target_pairs={{2,0},{3,1},{4,2},{5,3},{6,4},{7,5},{8,6},{9,7},{10,8},{11,9},{12,... | collective-permute-start | bytes 466952 | tf_op jit(solution)/shard_map/ppermute | solution.py:281
  25.9 15.7 %collective-permute-start.6 = (bf16[304,256]{1,0:T(8,128)(2,1)S(1)}, bf16[304,256]{1,0:T(8,128)(2,1)S(1)}, u32[]{:S(2)}, u32[]{:S(2)}) collective-permute-start(bf16[304,256]{1,0:T(8,128)(2,1)S(1)} %assemble.1.refs_0_), channel_id=1, source_target_pairs={{1,0},{2,1},{3,2},{4,3},{5,4},{6,5},{7,6},{8,7},{9,8},{10,9},{11,1... | collective-permute-start | bytes 466952 | tf_op jit(solution)/shard_map/ppermute | solution.py:281
  26.6 15.0 %collective-permute-start.9 = (bf16[304,256]{1,0:T(8,128)(2,1)S(1)}, bf16[304,256]{1,0:T(8,128)(2,1)S(1)}, u32[]{:S(2)}, u32[]{:S(2)}) collective-permute-start(bf16[304,256]{1,0:T(8,128)(2,1)S(1)} %collective-permute-done.8.rest_1_), channel_id=1, source_target_pairs={{30,0},{31,1},{0,2},{1,3},{2,4},{3,5},{4,6},{5,7},{6,8},{7,9},{8,1... | collective-permute-start | bytes 466952 | tf_op jit(solution)/shard_map/ppermute | solution.py:281
  28.2 13.6 %collective-permute-start.11 = (bf16[304,256]{1,0:T(8,128)(2,1)S(1)}, bf16[304,256]{1,0:T(8,128)(2,1)S(1)}, u32[]{:S(2)}, u32[]{:S(2)}) collective-permute-start(bf16[304,256]{1,0:T(8,128)(2,1)S(1)} %collective-permute-done.7.rest_0_.refs_2_), channel_id=1, source_target_pairs={{2,0},{3,1},{4,2},{5,3},{6,4},{7,5},{8,6},{9,7},{10,8},{11,9},{12,... | collective-permute-start | bytes 466952 | tf_op jit(solution)/shard_map/ppermute | solution.py:281
  35.0 8.8 %collective-permute-start.13 = (bf16[304,256]{1,0:T(8,128)(2,1)S(1)}, bf16[304,256]{1,0:T(8,128)(2,1)S(1)}, u32[]{:S(2)}, u32[]{:S(2)}) collective-permute-start(bf16[304,256]{1,0:T(8,128)(2,1)S(1)} %collective-permute-done.8.rest_1_), channel_id=1, source_target_pairs={{31,0},{0,1},{1,2},{2,3},{3,4},{4,5},{5,6},{6,7},{7,8},{8,9},{9,10... | collective-permute-start | bytes 466952 | tf_op jit(solution)/shard_map/ppermute | solution.py:281
  39.3 7.2 %collective-permute-start.10 = (bf16[304,256]{1,0:T(8,128)(2,1)S(1)}, bf16[304,256]{1,0:T(8,128)(2,1)S(1)}, u32[]{:S(2)}, u32[]{:S(2)}) collective-permute-start(bf16[304,256]{1,0:T(8,128)(2,1)S(1)} %collective-permute-done.7.rest_0_.refs_2_), channel_id=1, source_target_pairs={{1,0},{2,1},{3,2},{4,3},{5,4},{6,5},{7,6},{8,7},{9,8},{10,9},{11,1... | collective-permute-start | bytes 466952 | tf_op jit(solution)/shard_map/ppermute | solution.py:281
  41.6 8.0 %collective-permute-start.14 = (bf16[304,256]{1,0:T(8,128)(2,1)S(1)}, bf16[304,256]{1,0:T(8,128)(2,1)S(1)}, u32[]{:S(2)}, u32[]{:S(2)}) collective-permute-start(bf16[304,256]{1,0:T(8,128)(2,1)S(1)} %collective-permute-done.6.rest_0_.refs_1_), channel_id=1, source_target_pairs={{8,0},{9,1},{10,2},{11,3},{12,4},{13,5},{14,6},{15,7},{16,8},{17,9... | collective-permute-start | bytes 466952 | tf_op jit(solution)/shard_map/ppermute | solution.py:281
  41.6 8.0 %collective-permute-start.12 = (bf16[304,256]{1,0:T(8,128)(2,1)S(1)}, bf16[304,256]{1,0:T(8,128)(2,1)S(1)}, u32[]{:S(2)}, u32[]{:S(2)}) collective-permute-start(bf16[304,256]{1,0:T(8,128)(2,1)S(1)} %collective-permute-done.9.rest_1_.refs_6_), channel_id=1, source_target_pairs={{31,0},{0,1},{1,2},{2,3},{3,4},{4,5},{5,6},{6,7},{7,8},{8,9},{9,10... | collective-permute-start | bytes 466952 | tf_op jit(solution)/shard_map/ppermute | solution.py:281
  41.7 7.9 %collective-permute-start.15 = (bf16[304,256]{1,0:T(8,128)(2,1)S(1)}, bf16[304,256]{1,0:T(8,128)(2,1)S(1)}, u32[]{:S(2)}, u32[]{:S(2)}) collective-permute-start(bf16[304,256]{1,0:T(8,128)(2,1)S(1)} %collective-permute-done.7.rest_0_.refs_2_), channel_id=1, source_target_pairs={{8,0},{9,1},{10,2},{11,3},{12,4},{13,5},{14,6},{15,7},{16,8},{17,9... | collective-permute-start | bytes 466952 | tf_op jit(solution)/shard_map/ppermute | solution.py:281

commit v2 on v0

--- a/solution.py
+++ b/solution.py
@@ -73,19 +73,23 @@
     return slopes, k_part, v_part
 
 
-def pack_body(start, q, g, k, v, vq, vg, out, msg, buf, sems):
+def pack_body(start, q, g, k, v, vq, vg, out, msg, sems):
     copies = [
-        pltpu.make_async_copy(ref, buf.at[n], sems.at[n]) for n, ref in enumerate((q, g, k, v))
+        pltpu.make_async_copy(
+            ref.at[:, h * PAIR : (h + 1) * PAIR],
+            out.at[h, :, n * PAIR : (n + 1) * PAIR],
+            sems.at[n, h],
+        )
+        for n, ref in enumerate((q, g, k, v))
+        for h in range(out.shape[0])
     ]
     for copy in copies:
         copy.start()
     top = jnp.concatenate([vq[...], vg[...]], 1).astype(F32)
     low = jnp.full((8, 2 * PAIR), start[0].astype(F32))
     msg[...] = jnp.concatenate([top, low], 0).astype(BF16)
-    for n, copy in enumerate(copies):
+    for copy in copies:
         copy.wait()
-        for h in range(out.shape[0]):
-            out[h, :, n * PAIR : (n + 1) * PAIR] = buf[n, :, h * PAIR : (h + 1) * PAIR]
 
 
 def unpack_body(x, qo, ko, vo):
@@ -294,8 +298,8 @@
             jax.ShapeDtypeStruct((heads, rows, 4 * PAIR), BF16),
             jax.ShapeDtypeStruct((16, 2 * PAIR), BF16),
         ),
-        [SMEM] + [anywhere] * 4 + [VMEM] * 2, (VMEM, VMEM), 1 << 20,
-        scratch=(pltpu.VMEM((4, rows, heads * PAIR), BF16), pltpu.SemaphoreType.DMA((4,))),
+        [SMEM] + [anywhere] * 4 + [VMEM] * 2, (anywhere, VMEM), 1 << 20,
+        scratch=(pltpu.SemaphoreType.DMA((4, heads)),),
         name="pack", vmem=60,
     )(start, queries, out_grad, keys, values, variant_queries, variant_grads)
     msgs = [msg] + [shift(msg, ROW * d) for d in range(1, COLS)]
@@ -322,7 +326,7 @@
         ),
         aliases={3: 0}, name="state",
     )(start, prefix_state[0], t, acc)
-    near, second, acc = lax.optimization_barrier((blocks[1], blocks[2], acc))
+    near, second = lax.optimization_barrier((blocks[1], blocks[2]))
     blocks[9], blocks[10] = shift(near, ROW), shift(second, ROW)
     done = ((1, 8), (2, 7), (4, 5))
     parts = [later_call(fars, start, t, [blocks[far] for far in fars]) for fars in done]

time: 65.9 us -> 71.7 us (1.088)
  Pallas kernels: 10.5 us -> 17.7 us
  waiting for transfers between devices: 8.29 us -> 7.1 us
    pallas_call x1, Pallas kernels: 2.4 us -> 10.6 us  [body(): call(pack_body, (jax.ShapeDtypeStruct((heads, rows, 4 * PAIR), BF16), jax...]
    ppermute x13, waiting for transfers between devices: 7.61 us -> 6.42 us  [shift(): lax.ppermute(x, 'seq', [((i + d) % SHARDS, i) for i in range(SHARDS)])]
    pallas_call x1, Pallas kernels: 2.45 us -> 1.39 us  [body(): call(functools.partial(final_body, done, left), (ACC, jax.ShapeDtypeStruc...]
  transfers between devices with their start and end apart: 14 -> 14, of which waited for: 5 -> 4; matrix products, arithmetic and copies ran while one was open for 0% -> 0% of each run, Pallas kernels for 7% -> 7%
where the time goes in v2:
time: 71.7 us; the launch traced here: 71.4 us
  starting transfers between devices  32.5 us (45%)
  Pallas kernels  17.7 us (25%)
  blocking collectives  12 us (17%)
  waiting for transfers between devices  7.1 us (10%)
  between operations  2.09 us (3%)
    ppermute x13, starting transfers between devices, shift(): lax.ppermute(x, 'seq', [((i + d) % SHARDS, i) for i in range(SHARDS)])  25.8 us
    all_to_all x1, blocking collectives, body(): lax.all_to_all(small.reshape(heads, rows, 3 * PAIR), 'heads', split_axis=...  12 us
    pallas_call x1, Pallas kernels, body(): call(pack_body, (jax.ShapeDtypeStruct((heads, rows, 4 * PAIR), BF16), jax...  10.6 us
    all_to_all x1, starting transfers between devices, body(): lax.all_to_all(sent, 'heads', split_axis=0, concat_axis=0)  6.7 us
    ppermute x13, waiting for transfers between devices, shift(): lax.ppermute(x, 'seq', [((i + d) % SHARDS, i) for i in range(SHARDS)])  6.42 us
    pallas_call x3, Pallas kernels, later_call(): call(functools.partial(later_body, fars), jax.ShapeDtypeStruct((len(fars)...  2.56 us
    pallas_call x1, Pallas kernels, body(): call(state_body, ACC, [SMEM, VMEM, VMEM, VMEM], VMEM, 3 * BLOCK_FLOPS, sc...  1.71 us
  transfers between devices with their start and end apart: 14, of which 4 were waited for; matrix products, arithmetic and copies ran while one was open for 0% of the time, Pallas kernels for 7%

profile of v2, /device:TPU:1, one launch (start us, length us, event | category | flops | bytes accessed | tf_op | source)
XLA Modules:
  0.0 71.4 jit_solution(4055823533697025460)
XLA Ops:
  1.3 10.6 %pack.1 = (bf16[8,32,512]{2,1,0:T(8,128)(2,1)}, bf16[16,256]{1,0:T(8,128)(2,1)}) custom-call(s32[1]{0:T(128)S(6)} %copy.52.start.start_ref, bf16[32,1024]{1,0:T(8,128)(2,1)} %q.1, bf16[32,1024]{1,0:T(8,128)(2,1)} %g.1, bf16[32,1024]{1,0:T(8,128)(2,1)} %k.1, bf16[32,1024]{1,0:T(8,128)(2,1)} %v.1, bf16[8,128]{1,0:T(8,128)(2,1)} %vq.1, bf16[8,128]{1,0:T(8,128)(2,1)} %vg.1), custom_call_target="tpu_custom_call" | custom-call | flops 1048576 | bytes 1048576 | tf_op jit(solution)/shard_map/pack/pallas_call | solution.py:295
  11.9 0.0 copy-start.1
  11.9 0.0 copy-start.2
  11.9 0.0 copy-start.3
  12.0 6.7 %all-to-all-start = ((bf16[8,32,512]{2,1,0:T(8,128)(2,1)}), bf16[8,32,512]{2,1,0:T(8,128)(2,1)S(1)}, u32[]{:S(2)}, u32[]{:S(2)}) async-start(bf16[8,32,512]{2,1,0:T(8,128)(2,1)} %get-tuple-element.129), calls=%async_computation | async-start | bytes 524288 | tf_op jit(solution)/shard_map/all_to_all | solution.py:306
  18.7 0.0 copy-done.1
  18.7 0.6 collective-permute-start.6
  19.3 2.5 %collective-permute-start.5 = (bf16[16,256]{1,0:T(8,128)(2,1)S(1)}, bf16[16,256]{1,0:T(8,128)(2,1)S(1)}, u32[]{:S(2)}, u32[]{:S(2)}) collective-permute-start(bf16[16,256]{1,0:T(8,128)(2,1)S(1)} %copy-done.1), channel_id=1, source_target_pairs={{16,0},{17,1},{18,2},{19,3},{20,4},{21,5},{22,6},{23,7},{24,8},{25... | collective-permute-start | bytes 24584 | tf_op jit(solution)/shard_map/ppermute | solution.py:285
  21.7 1.2 %collective-permute-start.4 = (bf16[16,256]{1,0:T(8,128)(2,1)S(1)}, bf16[16,256]{1,0:T(8,128)(2,1)S(1)}, u32[]{:S(2)}, u32[]{:S(2)}) collective-permute-start(bf16[16,256]{1,0:T(8,128)(2,1)S(1)} %copy-done.1), channel_id=1, source_target_pairs={{8,0},{9,1},{10,2},{11,3},{12,4},{13,5},{14,6},{15,7},{16,8},{17,9... | collective-permute-start | bytes 24584 | tf_op jit(solution)/shard_map/ppermute | solution.py:285
  22.9 0.0 collective-permute-done.6.rest_3_
  22.9 0.5 collective-permute-done.5.rest_2_
  23.4 1.1 %collective-permute-done.4.rest_1_ = bf16[16,256]{1,0:T(8,128)(2,1)S(1)} collective-permute-done((bf16[16,256]{1,0:T(8,128)(2,1)S(1)}, bf16[16,256]{1,0:T(8,128)(2,1)S(1)}, u32[]{:S(2)}, u32[]{:S(2)}) %collective-permute-start.4) | collective-permute-done | bytes 8224 | tf_op jit(solution)/shard_map/ppermute | solution.py:285
  24.5 0.7 all-to-all-done
  25.2 0.0 copy-start
  25.2 3.3 %collective-permute-start.11 = (bf16[304,256]{1,0:T(8,128)(2,1)S(1)}, bf16[304,256]{1,0:T(8,128)(2,1)S(1)}, u32[]{:S(2)}, u32[]{:S(2)}) collective-permute-start(bf16[304,256]{1,0:T(8,128)(2,1)S(1)} %assemble.1.refs_0_), channel_id=1, source_target_pairs={{7,0},{8,1},{9,2},{10,3},{11,4},{12,5},{13,6},{14,7},{15,8},{16,9}... | collective-permute-start | bytes 466952 | tf_op jit(solution)/shard_map/ppermute | solution.py:285
  28.5 5.4 %collective-permute-start.8 = (bf16[304,256]{1,0:T(8,128)(2,1)S(1)}, bf16[304,256]{1,0:T(8,128)(2,1)S(1)}, u32[]{:S(2)}, u32[]{:S(2)}) collective-permute-start(bf16[304,256]{1,0:T(8,128)(2,1)S(1)} %assemble.1.refs_0_), channel_id=1, source_target_pairs={{2,0},{3,1},{4,2},{5,3},{6,4},{7,5},{8,6},{9,7},{10,8},{11,9},{12,... | collective-permute-start | bytes 466952 | tf_op jit(solution)/shard_map/ppermute | solution.py:285
  33.9 0.7 %collective-permute-start.7 = (bf16[304,256]{1,0:T(8,128)(2,1)S(1)}, bf16[304,256]{1,0:T(8,128)(2,1)S(1)}, u32[]{:S(2)}, u32[]{:S(2)}) collective-permute-start(bf16[304,256]{1,0:T(8,128)(2,1)S(1)} %assemble.1.refs_0_), channel_id=1, source_target_pairs={{1,0},{2,1},{3,2},{4,3},{5,4},{6,5},{7,6},{8,7},{9,8},{10,9},{11,1... | collective-permute-start | bytes 466952 | tf_op jit(solution)/shard_map/ppermute | solution.py:285
  34.6 0.3 collective-permute-start.14
  34.9 0.0 collective-permute-done.11.rest_1_.refs_7_
  34.9 0.6 collective-permute-start.12
  35.5 4.8 %collective-permute-done.8.rest_0_.refs_2_ = bf16[304,256]{1,0:T(8,128)(2,1)S(1)} collective-permute-done((bf16[304,256]{1,0:T(8,128)(2,1)S(1)}, bf16[304,256]{1,0:T(8,128)(2,1)S(1)}, u32[]{:S(2)}, u32[]{:S(2)}) %collective-permute-start.8) | collective-permute-done | bytes 155680 | tf_op jit(solution)/shard_map/ppermute | solution.py:285
  40.3 6.6 %collective-permute-start.10 = (bf16[304,256]{1,0:T(8,128)(2,1)S(1)}, bf16[304,256]{1,0:T(8,128)(2,1)S(1)}, u32[]{:S(2)}, u32[]{:S(2)}) collective-permute-start(bf16[304,256]{1,0:T(8,128)(2,1)S(1)} %collective-permute-done.8.rest_0_.refs_2_), channel_id=1, source_target_pairs={{2,0},{3,1},{4,2},{5,3},{6,4},{7,5},{8,6},{9,7},{10,8},{11,9},{12,... | collective-permute-start | bytes 466952 | tf_op jit(solution)/shard_map/ppermute | solution.py:285
  46.8 0.0 collective-permute-done.7.rest_0_.refs_1_
  46.8 0.0 collective-permute-start.15
  46.8 0.0 collective-permute-start.13
  46.9 0.0 collective-permute-done.14.rest_1_
  46.9 4.8 %collective-permute-start.9 = (bf16[304,256]{1,0:T(8,128)(2,1)S(1)}, bf16[304,256]{1,0:T(8,128)(2,1)S(1)}, u32[]{:S(2)}, u32[]{:S(2)}) collective-permute-start(bf16[304,256]{1,0:T(8,128)(2,1)S(1)} %collective-permute-done.8.rest_0_.refs_2_), channel_id=1, source_target_pairs={{1,0},{2,1},{3,2},{4,3},{5,4},{6,5},{7,6},{8,7},{9,8},{10,9},{11,1... | collective-permute-start | bytes 466952 | tf_op jit(solution)/shard_map/ppermute | solution.py:285
  51.6 0.0 collective-permute-done.12.rest_1_.refs_5_
  51.6 0.0 collective-permute-start.16
  51.6 0.0 copy-done.2
  51.6 0.0 copy-done.3
  51.7 0.6 own.1
  52.2 0.0 copy-done
  52.2 1.7 %state.1.acc_in = f32[256,384]{1,0:T(8,128)S(1)} custom-call(s32[1]{0:T(128)S(6)} %copy.52.start.start_ref, bf16[2080,128]{1,0:T(8,128)(2,1)S(1)} %bitcast.9, bf16[256,512]{1,0:T(8,128)(2,1)S(1)} %bitcast.14, f32[256,384]{1,0:T(8,128)S(1)} %get-tuple-element.131.acc_in), custom_call_target="tpu_custom_call", output_to_operand_aliasing={{}: (3, {})} | custom-call | flops 402653184 | bytes 1048576 | tf_op jit(solution)/shard_map/state/pallas_call | solution.py:319
  54.0 0.8 %later.4.refs_9_ = f32[2,256,256]{2,1,0:T(8,128)S(1)} custom-call(s32[1]{0:T(128)S(6)} %copy.52.start.start_ref, bf16[256,512]{1,0:T(8,128)(2,1)S(1)} %bitcast.15, bf16[304,256]{1,0:T(8,128)(2,1)S(1)} %collective-permute-done.8.rest_0_.refs_2_, bf16[304,256]{1,0:T(8,128)(2,1)S(1)} %collective-permute-done.11.rest_1_.refs_7_), custom_call_target="tpu_custom_call" | custom-call | flops 268435456 | bytes 1048576 | tf_op jit(solution)/shard_map/later/pallas_call | solution.py:270
  54.8 0.9 %later.3.refs_8_ = f32[2,256,256]{2,1,0:T(8,128)S(1)} custom-call(s32[1]{0:T(128)S(6)} %copy.52.start.start_ref, bf16[256,512]{1,0:T(8,128)(2,1)S(1)} %bitcast.16, bf16[304,256]{1,0:T(8,128)(2,1)S(1)} %collective-permute-done.7.rest_0_.refs_1_, bf16[304,256]{1,0:T(8,128)(2,1)S(1)} %collective-permute-done.14.rest_1_), custom_call_target="tpu_custom_call" | custom-call | flops 268435456 | bytes 1048576 | tf_op jit(solution)/shard_map/later/pallas_call | solution.py:270
  55.7 0.0 collective-permute-done.10.rest_0_.refs_4_
  55.7 0.9 %later.5.refs_10_ = f32[2,256,256]{2,1,0:T(8,128)S(1)} custom-call(s32[1]{0:T(128)S(6)} %copy.52.start.start_ref, bf16[256,512]{1,0:T(8,128)(2,1)S(1)} %bitcast.17, bf16[304,256]{1,0:T(8,128)(2,1)S(1)} %collective-permute-done.10.rest_0_.refs_4_, bf16[304,256]{1,0:T(8,128)(2,1)S(1)} %collective-permute-done.12.rest_1_.refs_5_), custom_call_target="tpu_custom_call" | custom-call | flops 268435456 | bytes 1048576 | tf_op jit(solution)/shard_map/later/pallas_call | solution.py:270
  56.6 0.0 collective-permute-done.13.refs_6_.refs_12_
  56.6 0.0 collective-permute-done.9.refs_3_.refs_11_
  56.6 0.0 collective-permute-done.15.refs_13_
  56.6 0.0 collective-permute-done.16.refs_14_
  56.6 1.4 %final.1 = (f32[256,384]{1,0:T(8,128)S(1)}, bf16[256,384]{1,0:T(8,128)(2,1)S(1)}, s32[1]{0:T(128)}, s32[1]{0:T(128)}) custom-call(s32[1]{0:T(128)S(6)} %copy.52.start.start_ref, s32[8,256]{1,0:T(8,128)S(1)} %get-tuple-element.130.who, bf16[256,512]{1,0:T(8,128)(2,1)S(1)} %bitcast.18, f32[256,384]{1,0:T(8,128)S(1)} %state.1.acc_in, ...), custom_call_target="tpu_custom_call", output_to_operand_aliasing={{0}: (3, {})} | custom-call | flops 134217728 | bytes 1048576 | tf_op jit(solution)/shard_map/final/pallas_call | solution.py:336
  58.7 12.0 %all_to_all.10.x = bf16[8,32,384]{2,1,0:T(8,128)(2,1)S(1)} all-to-all(bf16[8,32,384]{2,1,0:T(8,128)(2,1)S(1)} %bitcast.20), channel_id=1, replica_groups=mesh['heads'=8,'seq'=32] {'heads'}, dimensions={0} | all-to-all | bytes 393216 | tf_op jit(solution)/shard_map/all_to_all | solution.py:364
  70.6 0.8 %unpack.1 = (f32[32,1024]{1,0:T(8,128)}, f32[32,1024]{1,0:T(8,128)}, f32[32,1024]{1,0:T(8,128)}) custom-call(bf16[8,32,384]{2,1,0:T(8,128)(2,1)S(1)} %all_to_all.10.x), custom_call_target="tpu_custom_call" | custom-call | flops 1048576 | bytes 1048576 | tf_op jit(solution)/shard_map/unpack/pallas_call | solution.py:366
  (2 shorter events, 0.0 us)
Async XLA Ops:
  11.9 6.7 %copy-start.1 = (bf16[16,256]{1,0:T(8,128)(2,1)S(1)}, bf16[16,256]{1,0:T(8,128)(2,1)}, u32[]{:S(2)}) copy-start(bf16[16,256]{1,0:T(8,128)(2,1)} %get-tuple-element.132.rest_0_) | copy-start | bytes 24580
  11.9 39.7 %copy-start.2 = (s32[256]{0:T(256)S(1)}, s32[256]{0:T(256)}, u32[]{:S(2)}) copy-start(s32[256]{0:T(256)} %param.21) | copy-start | bytes 3076
  11.9 39.7 %copy-start.3 = (s32[256]{0:T(256)S(1)}, s32[256]{0:T(256)}, u32[]{:S(2)}) copy-start(s32[256]{0:T(256)} %param.22) | copy-start | bytes 3076
  12.0 13.2 %all-to-all-start = ((bf16[8,32,512]{2,1,0:T(8,128)(2,1)}), bf16[8,32,512]{2,1,0:T(8,128)(2,1)S(1)}, u32[]{:S(2)}, u32[]{:S(2)}) async-start(bf16[8,32,512]{2,1,0:T(8,128)(2,1)} %get-tuple-element.129), calls=%async_computation | async-start | bytes 524288 | tf_op jit(solution)/shard_map/all_to_all | solution.py:306
  18.7 4.3 %collective-permute-start.6 = (bf16[16,256]{1,0:T(8,128)(2,1)S(1)}, bf16[16,256]{1,0:T(8,128)(2,1)S(1)}, u32[]{:S(2)}, u32[]{:S(2)}) collective-permute-start(bf16[16,256]{1,0:T(8,128)(2,1)S(1)} %copy-done.1), channel_id=1, source_target_pairs={{24,0},{25,1},{26,2},{27,3},{28,4},{29,5},{30,6},{31,7},{0,8},{1,9... | collective-permute-start | bytes 24584 | tf_op jit(solution)/shard_map/ppermute | solution.py:285
  19.3 4.1 %collective-permute-start.5 = (bf16[16,256]{1,0:T(8,128)(2,1)S(1)}, bf16[16,256]{1,0:T(8,128)(2,1)S(1)}, u32[]{:S(2)}, u32[]{:S(2)}) collective-permute-start(bf16[16,256]{1,0:T(8,128)(2,1)S(1)} %copy-done.1), channel_id=1, source_target_pairs={{16,0},{17,1},{18,2},{19,3},{20,4},{21,5},{22,6},{23,7},{24,8},{25... | collective-permute-start | bytes 24584 | tf_op jit(solution)/shard_map/ppermute | solution.py:285
  21.7 2.7 %collective-permute-start.4 = (bf16[16,256]{1,0:T(8,128)(2,1)S(1)}, bf16[16,256]{1,0:T(8,128)(2,1)S(1)}, u32[]{:S(2)}, u32[]{:S(2)}) collective-permute-start(bf16[16,256]{1,0:T(8,128)(2,1)S(1)} %copy-done.1), channel_id=1, source_target_pairs={{8,0},{9,1},{10,2},{11,3},{12,4},{13,5},{14,6},{15,7},{16,8},{17,9... | collective-permute-start | bytes 24584 | tf_op jit(solution)/shard_map/ppermute | solution.py:285
  25.2 27.1 %copy-start = (bf16[1,2080,128]{2,1,0:T(8,128)(2,1)S(1)}, bf16[1,2080,128]{2,1,0:T(8,128)(2,1)}, u32[]{:S(2)}) copy-start(bf16[1,2080,128]{2,1,0:T(8,128)(2,1)} %param.18) | copy-start | bytes 1597444
  25.2 9.7 %collective-permute-start.11 = (bf16[304,256]{1,0:T(8,128)(2,1)S(1)}, bf16[304,256]{1,0:T(8,128)(2,1)S(1)}, u32[]{:S(2)}, u32[]{:S(2)}) collective-permute-start(bf16[304,256]{1,0:T(8,128)(2,1)S(1)} %assemble.1.refs_0_), channel_id=1, source_target_pairs={{7,0},{8,1},{9,2},{10,3},{11,4},{12,5},{13,6},{14,7},{15,8},{16,9}... | collective-permute-start | bytes 466952 | tf_op jit(solution)/shard_map/ppermute | solution.py:285
  28.5 11.8 %collective-permute-start.8 = (bf16[304,256]{1,0:T(8,128)(2,1)S(1)}, bf16[304,256]{1,0:T(8,128)(2,1)S(1)}, u32[]{:S(2)}, u32[]{:S(2)}) collective-permute-start(bf16[304,256]{1,0:T(8,128)(2,1)S(1)} %assemble.1.refs_0_), channel_id=1, source_target_pairs={{2,0},{3,1},{4,2},{5,3},{6,4},{7,5},{8,6},{9,7},{10,8},{11,9},{12,... | collective-permute-start | bytes 466952 | tf_op jit(solution)/shard_map/ppermute | solution.py:285
  33.9 12.9 %collective-permute-start.7 = (bf16[304,256]{1,0:T(8,128)(2,1)S(1)}, bf16[304,256]{1,0:T(8,128)(2,1)S(1)}, u32[]{:S(2)}, u32[]{:S(2)}) collective-permute-start(bf16[304,256]{1,0:T(8,128)(2,1)S(1)} %assemble.1.refs_0_), channel_id=1, source_target_pairs={{1,0},{2,1},{3,2},{4,3},{5,4},{6,5},{7,6},{8,7},{9,8},{10,9},{11,1... | collective-permute-start | bytes 466952 | tf_op jit(solution)/shard_map/ppermute | solution.py:285
  34.6 12.2 %collective-permute-start.14 = (bf16[304,256]{1,0:T(8,128)(2,1)S(1)}, bf16[304,256]{1,0:T(8,128)(2,1)S(1)}, u32[]{:S(2)}, u32[]{:S(2)}) collective-permute-start(bf16[304,256]{1,0:T(8,128)(2,1)S(1)} %assemble.1.refs_0_), channel_id=1, source_target_pairs={{8,0},{9,1},{10,2},{11,3},{12,4},{13,5},{14,6},{15,7},{16,8},{17,9... | collective-permute-start | bytes 466952 | tf_op jit(solution)/shard_map/ppermute | solution.py:285
  34.9 16.7 %collective-permute-start.12 = (bf16[304,256]{1,0:T(8,128)(2,1)S(1)}, bf16[304,256]{1,0:T(8,128)(2,1)S(1)}, u32[]{:S(2)}, u32[]{:S(2)}) collective-permute-start(bf16[304,256]{1,0:T(8,128)(2,1)S(1)} %collective-permute-done.11.rest_1_.refs_7_), channel_id=1, source_target_pairs={{30,0},{31,1},{0,2},{1,3},{2,4},{3,5},{4,6},{5,7},{6,8},{7,9},{8,1... | collective-permute-start | bytes 466952 | tf_op jit(solution)/shard_map/ppermute | solution.py:285
  40.3 15.4 %collective-permute-start.10 = (bf16[304,256]{1,0:T(8,128)(2,1)S(1)}, bf16[304,256]{1,0:T(8,128)(2,1)S(1)}, u32[]{:S(2)}, u32[]{:S(2)}) collective-permute-start(bf16[304,256]{1,0:T(8,128)(2,1)S(1)} %collective-permute-done.8.rest_0_.refs_2_), channel_id=1, source_target_pairs={{2,0},{3,1},{4,2},{5,3},{6,4},{7,5},{8,6},{9,7},{10,8},{11,9},{12,... | collective-permute-start | bytes 466952 | tf_op jit(solution)/shard_map/ppermute | solution.py:285
  46.8 9.7 %collective-permute-start.15 = (bf16[304,256]{1,0:T(8,128)(2,1)S(1)}, bf16[304,256]{1,0:T(8,128)(2,1)S(1)}, u32[]{:S(2)}, u32[]{:S(2)}) collective-permute-start(bf16[304,256]{1,0:T(8,128)(2,1)S(1)} %collective-permute-done.7.rest_0_.refs_1_), channel_id=1, source_target_pairs={{8,0},{9,1},{10,2},{11,3},{12,4},{13,5},{14,6},{15,7},{16,8},{17,9... | collective-permute-start | bytes 466952 | tf_op jit(solution)/shard_map/ppermute | solution.py:285
  46.8 9.7 %collective-permute-start.13 = (bf16[304,256]{1,0:T(8,128)(2,1)S(1)}, bf16[304,256]{1,0:T(8,128)(2,1)S(1)}, u32[]{:S(2)}, u32[]{:S(2)}) collective-permute-start(bf16[304,256]{1,0:T(8,128)(2,1)S(1)} %collective-permute-done.11.rest_1_.refs_7_), channel_id=1, source_target_pairs={{31,0},{0,1},{1,2},{2,3},{3,4},{4,5},{5,6},{6,7},{7,8},{8,9},{9,10... | collective-permute-start | bytes 466952 | tf_op jit(solution)/shard_map/ppermute | solution.py:285
  46.9 9.7 %collective-permute-start.9 = (bf16[304,256]{1,0:T(8,128)(2,1)S(1)}, bf16[304,256]{1,0:T(8,128)(2,1)S(1)}, u32[]{:S(2)}, u32[]{:S(2)}) collective-permute-start(bf16[304,256]{1,0:T(8,128)(2,1)S(1)} %collective-permute-done.8.rest_0_.refs_2_), channel_id=1, source_target_pairs={{1,0},{2,1},{3,2},{4,3},{5,4},{6,5},{7,6},{8,7},{9,8},{10,9},{11,1... | collective-permute-start | bytes 466952 | tf_op jit(solution)/shard_map/ppermute | solution.py:285
  51.6 5.0 %collective-permute-start.16 = (bf16[304,256]{1,0:T(8,128)(2,1)S(1)}, bf16[304,256]{1,0:T(8,128)(2,1)S(1)}, u32[]{:S(2)}, u32[]{:S(2)}) collective-permute-start(bf16[304,256]{1,0:T(8,128)(2,1)S(1)} %collective-permute-done.8.rest_0_.refs_2_), channel_id=1, source_target_pairs={{8,0},{9,1},{10,2},{11,3},{12,4},{13,5},{14,6},{15,7},{16,8},{17,9... | collective-permute-start | bytes 466952 | tf_op jit(solution)/shard_map/ppermute | solution.py:285
